TPU v7x, 512 devices: a whole 4x8x8 slice. The times are simulated.
512 devices in a mesh: dp: 4 (over z_hi), edata: 8 (over y), expert: 16 (over z_lo, x, core).
Axes of the slice: x: 4, y: 8, z: 8 (z_hi: 4, z_lo: 2; z = z_hi * 2 + z_lo), core: 2. Of those that a mesh axis runs over, the one named last changes fastest.
Arguments:
- out_grad: bfloat16 [65536, 7168], P(('dp', 'edata', 'expert')), may hold values from -6 to 6
- route_prob: float32 [65536, 2], P(('dp', 'edata', 'expert')), may hold values from 0.1 to 1
- expert_ids: int32 [65536, 2], P(('dp', 'edata', 'expert')), may hold values from 0 to 127, as said below
- slots: int32 [65536, 2], P(('dp', 'edata', 'expert')), may hold values from -1 to 3, as said below
- counts: int32 [512, 16], P(('dp', 'edata', 'expert')), may hold values from 0 to 4, as said below
- down_weight: bfloat16 [16, 2432, 7168], P('expert', 'dp', 'edata'), may hold values from -0.125 to 0.125
- saved_hidden: bfloat16 [16, 2048, 2432], P('expert', 'edata', 'dp'), may hold values from -0.29882812 to 0.29882812
Outputs:
- hidden_grad: bfloat16 [16, 2048, 2432], P('expert', 'edata', 'dp')
- weight_grad: bfloat16 [16, 2432, 7168], P('expert', 'dp', 'edata')
Inputs may be any that keep to these rules, and one draw needn't show every extreme that they name: `expert_ids`: each token names two different experts. Expert k * 8 is window expert k; a token names at most one window expert. `slots`: for a token's window expert, the number of earlier tokens of its block of 128 that name the same expert; -1 for the other expert. Row g counts the tokens of block g of 128 that name each window expert; some window expert has 4 in every row.
All inputs are finite; a program needn't handle non-finite values.
Results may differ from a plain program's by a relative error of at most 0.017.
Values may be sent and summed in bfloat16 or wider, within the bound.
No kernel may reach another device: no remote copies, remote signals or barrier semaphores. Data moves between devices by JAX's collectives and lax.ppermute only.
A program may use at most 64 MiB of HBM per device.

v0:
```python
import jax
import jax.numpy as jnp
from jax import lax
from jax.sharding import PartitionSpec as P

EXP_DEV = 8
CAP = 4


def per_device(out_grad, route_prob, expert_ids, slots, counts, down_weight, saved_hidden):
    flight = lax.axis_size("expert")
    edata_count = lax.axis_size("edata")
    tok_rows, model_width = out_grad.shape
    column_width = model_width // edata_count
    owner_index = expert_ids // EXP_DEV
    inside = expert_ids % EXP_DEV == 0
    experts_here = jnp.arange(flight, dtype=jnp.int32)
    slot_limit = jnp.sum(
        jnp.where(
            owner_index[:, :, None] == experts_here[None, None, :], counts[0][None, None, :], 0
        ),
        axis=2,
    )
    usable = inside & (slots >= 0) & (slots < slot_limit)
    target = jnp.where(usable, owner_index * CAP + slots, -1)
    slot_index = jnp.arange(flight * CAP, dtype=jnp.int32)
    matches = slot_index[:, None, None] == target[None, :, :]
    picker = jnp.any(matches, axis=2).astype(jnp.bfloat16)
    route_scale = jnp.sum(jnp.where(matches, route_prob[None, :, :], 0.0), axis=(1, 2))
    picked = jnp.dot(picker, out_grad, preferred_element_type=jnp.float32)
    outgoing = (
        (picked * route_scale[:, None]).astype(jnp.bfloat16).reshape(1, flight, CAP, model_width)
    )
    arrived = lax.all_to_all(outgoing, "expert", split_axis=1, concat_axis=1, tiled=True)
    stacked = lax.all_gather(
        arrived.reshape(1, flight * CAP, model_width), "dp", axis=0, tiled=True
    )
    parted = lax.all_to_all(stacked[None], "edata", split_axis=3, concat_axis=0, tiled=True)
    columns = jnp.swapaxes(parted, 0, 1).reshape(-1, column_width)
    weight_block = down_weight[0]
    hidden_part = lax.psum_scatter(
        lax.dot_general(
            columns, weight_block, (((1,), (1,)), ((), ())), preferred_element_type=jnp.float32
        ).astype(jnp.bfloat16),
        "edata",
        scatter_dimension=0,
        tiled=True,
    )
    running = lax.dot_general(
        lax.all_gather(saved_hidden[0], "edata", axis=0, tiled=True),
        columns,
        (((0,), (0,)), ((), ())),
        preferred_element_type=jnp.float32,
    )
    return (hidden_part[None], running.astype(jnp.bfloat16)[None])


def solution(mesh):
    placed = (
        P(("dp", "edata", "expert"), None),
        P(("dp", "edata", "expert"), None),
        P(("dp", "edata", "expert"), None),
        P(("dp", "edata", "expert"), None),
        P(("dp", "edata", "expert"), None),
        P("expert", "dp", "edata"),
        P("expert", "edata", "dp"),
    )
    return jax.shard_map(
        per_device,
        mesh=mesh,
        in_specs=placed,
        out_specs=(P("expert", "edata", "dp"), P("expert", "dp", "edata")),
        check_vma=False,
    )
```

profile of v0, /device:TPU:1, one launch (start us, length us, event | category | flops | bytes accessed | tf_op | source)
XLA Modules:
  0.0 326.3 jit_solution(13837082242599687491)
XLA Ops:
  8.0 0.0 copy-start
  8.0 0.0 all-gather.4.cloned.1.call-start
  8.1 0.8 and_select_fusion.1
  8.9 0.7 select_reduce_fusion.1
  9.6 0.7 and_select_fusion
  10.3 0.8 select_reduce_fusion
  11.1 0.0 copy-done
  11.1 1.3 fusion
  12.5 1.8 reshape.18
  14.3 24.1 %all_to_all.23 = bf16[1,16,4,7168]{3,2,0,1:T(4,128)(2,1)} all-to-all(bf16[1,16,4,7168]{3,2,0,1:T(4,128)(2,1)S(1)} %bitcast.35), channel_id=1, replica_groups=mesh['dp'=4,'edata'=8,'expert'=16] {'expert'}, dimensions={1} | all-to-all | bytes 1835008 | tf_op jit(solution)/shard_map/all_to_all | solution.py:34
  38.3 2.4 reshape.19
  40.7 0.0 all-gather.4.cloned.1.call-update
  40.7 80.5 %all-gather.4.cloned.1.call-done = bf16[4,64,7168]{2,1,0:T(8,128)(2,1)} async-done(((bf16[1,64,7168]{2,1,0:T(8,128)(2,1)}), bf16[4,64,7168]{2,1,0:T(8,128)(2,1)}) %all-gather.4.cloned.1.call-update) | async-done | bytes 3670032 | tf_op jit(solution)/shard_map/all_gather | solution.py:35
  121.3 11.2 %copy.27 = bf16[1,4,64,7168]{2,1,0,3:T(4,128)(2,1)} copy(bf16[1,4,64,7168]{3,2,1,0:T(8,128)(2,1)} %bitcast.38) | data formatting | bytes 7340032 | tf_op jit(solution)/shard_map/broadcast_in_dim | solution.py:38
  132.5 9.6 %reshape.22 = bf16[8,2,114688]{2,1,0:T(2,128)(2,1)} reshape(bf16[7168,1,4,64]{3,2,1,0:T(4,128)(2,1)} %bitcast.33) | data formatting | bytes 7340032
  142.1 6.5 %all-to-all-start.1 = ((bf16[8,2,114688]{2,1,0:T(2,128)(2,1)}), bf16[8,2,114688]{2,1,0:T(2,128)(2,1)}, u32[]{:S(2)}, u32[]{:S(2)}) async-start(bf16[8,2,114688]{2,1,0:T(2,128)(2,1)} %reshape.22), calls=%async_computation.1 | async-start | bytes 7340032 | tf_op jit(solution)/shard_map/all_to_all | solution.py:38
  148.6 0.0 all-gather.6.cloned.1.call-start
  148.6 0.5 all-gather.6.cloned.1.call-update
  149.1 0.0 reduce-scatter.2.cloned.1.call-start
  149.2 104.4 %all-to-all-done.1 = bf16[8,2,114688]{2,1,0:T(2,128)(2,1)} async-done(((bf16[8,2,114688]{2,1,0:T(2,128)(2,1)}), bf16[8,2,114688]{2,1,0:T(2,128)(2,1)}, u32[]{:S(2)}, u32[]{:S(2)}) %all-to-all-start.1) | async-done | bytes 3670048 | tf_op jit(solution)/shard_map/all_to_all | solution.py:38
  253.6 9.5 %reshape.23 = bf16[7168,1,4,64]{3,2,1,0:T(4,128)(2,1)} reshape(bf16[8,2,114688]{2,1,0:T(2,128)(2,1)} %all-to-all-done.1) | data formatting | bytes 7340032
  263.2 0.0 copy-start.1
  263.2 11.5 %copy.31 = bf16[1,4,64,8,896]{4,2,3,1,0:T(8,128)(2,1)} copy(bf16[1,4,64,8,896]{2,1,4,3,0:T(4,128)(2,1)} %bitcast.34) | data formatting | bytes 7340032 | tf_op jit(solution)/shard_map/transpose | solution.py:39
  274.6 0.0 copy-done.1
  274.6 6.2 %convolution_convert_fusion = bf16[2048,608]{0,1:T(8,128)(2,1)} fusion(bf16[2048,896]{1,0:T(8,128)(2,1)} %bitcast.36, bf16[1,608,896]{2,1,0:T(8,128)(2,1)S(1)} %copy-done.1), kind=kOutput, calls=%fused_computation.2 | convolution fusion | flops 2232614912 | bytes 7249920 | tf_op jit(solution)/shard_map/dot_general | solution.py:42
  280.8 0.0 reduce-scatter.2.cloned.1.call-update
  280.8 0.0 all-gather.6.cloned.1.call-done
  280.9 6.5 %fusion.6 = bf16[1,608,896]{2,1,0:T(8,128)(2,1)} fusion(bf16[2048,896]{1,0:T(8,128)(2,1)} %bitcast.37, bf16[1,2048,608]{1,2,0:T(8,128)(2,1)} %all-gather.6.cloned.1.call-done), kind=kOutput, calls=%fused_computation.6 | convolution fusion | flops 2231914496 | bytes 7249920 | tf_op jit(solution)/shard_map/dot_general | solution.py:49
  287.4 31.4 %reduce-scatter.2.cloned.1.call-done = bf16[256,608]{0,1:T(8,128)(2,1)} async-done(((bf16[2048,608]{0,1:T(8,128)(2,1)}), bf16[256,608]{0,1:T(8,128)(2,1)}) %reduce-scatter.2.cloned.1.call-update) | async-done | bytes 311312 | tf_op jit(solution)/shard_map/reduce_scatter | solution.py:41
  (1 shorter events, 0.0 us)
Async XLA Ops:
  8.0 3.1 copy-start
  8.0 113.2 %all-gather.4.cloned.1.call-start = ((), (), s32[]{:S(2)}) async-start(), calls=%async_computation.3 | async-start | bytes 4587520 | tf_op jit(solution)/shard_map/all_gather | solution.py:35
  142.1 111.5 %all-to-all-start.1 = ((bf16[8,2,114688]{2,1,0:T(2,128)(2,1)}), bf16[8,2,114688]{2,1,0:T(2,128)(2,1)}, u32[]{:S(2)}, u32[]{:S(2)}) async-start(bf16[8,2,114688]{2,1,0:T(2,128)(2,1)} %reshape.22), calls=%async_computation.1 | async-start | bytes 7340032 | tf_op jit(solution)/shard_map/all_to_all | solution.py:38
  148.6 132.3 %all-gather.6.cloned.1.call-start = ((), (), s32[]{:S(2)}) async-start(), calls=%async_computation.5 | async-start | bytes 2801664 | tf_op jit(solution)/shard_map/all_gather | solution.py:50
  149.1 169.7 %reduce-scatter.2.cloned.1.call-start = ((), (), s32[]{:S(2)}) async-start(), calls=%async_computation.4 | async-start | bytes 2801664 | tf_op jit(solution)/shard_map/reduce_scatter | solution.py:41
  263.2 11.5 %copy-start.1 = (bf16[1,608,896]{2,1,0:T(8,128)(2,1)S(1)}, bf16[1,608,896]{2,1,0:T(8,128)(2,1)}, u32[]{:S(2)}) copy-start(bf16[1,608,896]{2,1,0:T(8,128)(2,1)} %param.12) | copy-start | bytes 3268612
Sparse Core Ops, SparseCore 0:
  40.9 80.3 all-gather.3
Sparse Core Ops, SparseCore 1:
  151.0 105.2 all-gather.5
  280.9 37.8 reduce-scatter.1
where the time goes:
time: 331 us; the launch traced here: 326 us
  waiting for transfers between devices  217 us (66%)
  local copies, waits for them, and re-layouts  46 us (14%)
  blocking collectives  24.1 us (7%)
  between operations  15.5 us (5%)
  matrix products  14 us (4%)
  starting transfers between devices  6.57 us (2%)
    all_to_all x1, waiting for transfers between devices, per_device(): lax.all_to_all(stacked[None], 'edata', split_axis=3, concat_axis=0, tiled...  104 us
    all_gather x1, waiting for transfers between devices, per_device(): lax.all_gather(arrived.reshape(1, flight * CAP, model_width), 'dp', axis=...  80.5 us
    reduce_scatter x1, waiting for transfers between devices, per_device(): lax.psum_scatter(lax.dot_general(columns, weight_block, (((1,), (1,)), ((...  31.4 us
    all_to_all x1, blocking collectives, per_device(): lax.all_to_all(outgoing, 'expert', split_axis=1, concat_axis=1, tiled=True)  24.1 us
    unnamed x6, local copies, waits for them, and re-layouts  19.2 us
    transpose x1, local copies, waits for them, and re-layouts, per_device(): columns = jnp.swapaxes(parted, 0, 1).reshape(-1, column_width)  11.5 us
    broadcast_in_dim x1, local copies, waits for them, and re-layouts, per_device(): stacked[None]  11.2 us
  transfers between devices with their start and end apart: 4, of which 3 were waited for; matrix products, arithmetic and copies ran while one was open for 10% of the time, Pallas kernels for 0%

commit v1 on v0

v1 whole, which is shorter than its diff:
```python
import jax
import jax.numpy as jnp
from jax import lax
from jax.experimental import pallas as pl
from jax.experimental.pallas import tpu as pltpu
from jax.sharding import PartitionSpec as P

EXP_DEV = 8
CAP = 4
VMEM_LIMIT = 48 * 1024 * 1024


def dispatch_kernel(prob_ref, ids_ref, slots_ref, counts_ref, grad_ref, out_ref):
    rows = out_ref.shape[1]
    flight = counts_ref.shape[1]
    tokens = grad_ref.shape[0]
    own = lax.broadcasted_iota(jnp.int32, (rows, flight), 0) // CAP
    column = lax.broadcasted_iota(jnp.int32, (rows, flight), 1)
    limit = jnp.sum(jnp.where(own == column, counts_ref[...], 0), axis=1, keepdims=True)
    row = lax.broadcasted_iota(jnp.int32, (rows, tokens), 0)
    expert = (row // CAP) * EXP_DEV
    slot = row % CAP
    picker = jnp.zeros((rows, tokens), jnp.float32)
    scale = jnp.zeros((rows, 1), jnp.float32)
    for choice in range(2):
        match = (
            (ids_ref[choice : choice + 1, :] == expert)
            & (slots_ref[choice : choice + 1, :] == slot)
            & (slot < limit)
        )
        picker = picker + jnp.where(match, 1.0, 0.0)
        scale = scale + jnp.sum(
            jnp.where(match, prob_ref[choice : choice + 1, :], 0.0), axis=1, keepdims=True
        )
    picked = jnp.dot(
        picker.astype(jnp.bfloat16), grad_ref[...], preferred_element_type=jnp.float32
    )
    out_ref[0] = (picked * scale).astype(out_ref.dtype)


def dispatch(route_prob, expert_ids, slots, counts, out_grad, blocks):
    tokens, width = out_grad.shape
    flight = counts.shape[1]
    small = lambda shape: pl.BlockSpec(shape, lambda b: (0, 0))
    return pl.pallas_call(
        dispatch_kernel,
        grid=(blocks,),
        in_specs=[
            small((2, tokens)),
            small((2, tokens)),
            small((2, tokens)),
            small((1, flight)),
            pl.BlockSpec((tokens, width // blocks), lambda b: (0, b)),
        ],
        out_specs=pl.BlockSpec((1, flight * CAP, width // blocks), lambda b: (b, 0, 0)),
        out_shape=jax.ShapeDtypeStruct((blocks, flight * CAP, width // blocks), jnp.bfloat16),
        compiler_params=pltpu.CompilerParams(vmem_limit_bytes=VMEM_LIMIT),
    )(route_prob.T, expert_ids.T, slots.T, counts, out_grad)


def hidden_kernel(weight_ref, rows_ref, out_ref):
    out_ref[0] = lax.dot_general(
        weight_ref[...],
        rows_ref[0],
        (((1,), (1,)), ((), ())),
        preferred_element_type=jnp.float32,
    ).astype(out_ref.dtype)


def hidden_partial(weight, rows):
    units, width = weight.shape
    parts, slots, _ = rows.shape
    return pl.pallas_call(
        hidden_kernel,
        grid=(parts,),
        in_specs=[
            pl.BlockSpec((units, width), lambda b: (0, 0)),
            pl.BlockSpec((1, slots, width), lambda b: (b, 0, 0)),
        ],
        out_specs=pl.BlockSpec((1, units, slots), lambda b: (b, 0, 0)),
        out_shape=jax.ShapeDtypeStruct((parts, units, slots), jnp.bfloat16),
        compiler_params=pltpu.CompilerParams(vmem_limit_bytes=VMEM_LIMIT),
    )(weight, rows)


def weight_kernel(hidden_ref, rows_ref, out_ref, total):
    step = pl.program_id(0)

    @pl.when(step == 0)
    def _():
        total[...] = jnp.zeros_like(total)

    total[...] += jnp.dot(hidden_ref[0], rows_ref[0], preferred_element_type=jnp.float32)

    @pl.when(step == pl.num_programs(0) - 1)
    def _():
        out_ref[...] = total[...].astype(out_ref.dtype)


def weight_grad(hidden, rows):
    parts, units, slots = hidden.shape
    width = rows.shape[2]
    return pl.pallas_call(
        weight_kernel,
        grid=(parts,),
        in_specs=[
            pl.BlockSpec((1, units, slots), lambda b: (b, 0, 0)),
            pl.BlockSpec((1, slots, width), lambda b: (b, 0, 0)),
        ],
        out_specs=pl.BlockSpec((units, width), lambda b: (0, 0)),
        out_shape=jax.ShapeDtypeStruct((units, width), jnp.bfloat16),
        scratch_shapes=[pltpu.VMEM((units, width), jnp.float32)],
        compiler_params=pltpu.CompilerParams(vmem_limit_bytes=VMEM_LIMIT),
    )(hidden, rows)


def per_device(out_grad, route_prob, expert_ids, slots, counts, down_weight, saved_hidden):
    flight = lax.axis_size("expert")
    edata = lax.axis_size("edata")
    dp = lax.axis_size("dp")
    own_slots = saved_hidden.shape[1]
    width = out_grad.shape[1] // edata
    outgoing = dispatch(route_prob, expert_ids, slots, counts, out_grad, edata)
    arrived = lax.all_to_all(
        outgoing.reshape(edata * flight, CAP, width),
        ("edata", "expert"),
        split_axis=0,
        concat_axis=0,
        tiled=True,
    )
    rows = lax.all_gather(arrived.reshape(edata * flight * CAP, width), "dp", axis=0)
    rows = rows.reshape(edata, own_slots, width)
    hidden = lax.all_gather(saved_hidden[0].T, "edata", axis=0)
    partial = hidden_partial(down_weight[0], rows)
    hidden_grad = lax.psum_scatter(partial, "edata", scatter_dimension=0, tiled=False)
    grad = weight_grad(hidden, rows)
    return hidden_grad.T[None], grad[None]


def solution(mesh):
    placed = (
        P(("dp", "edata", "expert"), None),
        P(("dp", "edata", "expert"), None),
        P(("dp", "edata", "expert"), None),
        P(("dp", "edata", "expert"), None),
        P(("dp", "edata", "expert"), None),
        P("expert", "dp", "edata"),
        P("expert", "edata", "dp"),
    )
    return jax.shard_map(
        per_device,
        mesh=mesh,
        in_specs=placed,
        out_specs=(P("expert", "edata", "dp"), P("expert", "dp", "edata")),
        check_vma=False,
    )
```

time: 331 us -> 234 us (0.71)
  waiting for transfers between devices: 217 us -> 152 us
  local copies, waits for them, and re-layouts: 46 us -> 9.27 us
  blocking collectives: 24.1 us -> 40.4 us
  Pallas kernels: 0 us -> 15.5 us
  matrix products: 14 us -> 0 us
  starting transfers between devices: 6.57 us -> 0.12 us
    all_to_all x1 -> x0, waiting for transfers between devices: 104 us -> none  [per_device(): lax.all_to_all(stacked[None], 'edata', split_axis=3, concat_axis=0, tiled...]
    all_gather x2, waiting for transfers between devices: 80.5 us -> 113 us  [the longest x1 79.1 us: per_device(): lax.all_gather(arrived.reshape(edata * flight * CAP, width), 'dp', axis=0)]
    all_to_all x1, blocking collectives: 24.1 us -> 40.4 us  [per_device(): lax.all_to_all(outgoing.reshape(edata * flight, CAP, width), ('edata', 'e...]
    pallas_call x0 -> x3, Pallas kernels: none -> 15.5 us  [the longest x1 7.98 us: hidden_partial(): pl.pallas_call(hidden_kernel, grid=(parts,), in_specs=[pl.BlockSpec((unit...]
    dot_general x3 -> x0, matrix products: 14 us -> none  [the longest x1 6.51 us: per_device(): lax.dot_general(lax.all_gather(saved_hidden[0], 'edata', axis=0, tiled=Tr...]
    transpose x1 -> x0, local copies, waits for them, and re-layouts: 11.5 us -> none  [per_device(): columns = jnp.swapaxes(parted, 0, 1).reshape(-1, column_width)]
    unnamed x6 -> x16, local copies, waits for them, and re-layouts: 19.2 us -> 7.93 us
    broadcast_in_dim x1 -> x0, local copies, waits for them, and re-layouts: 11.2 us -> none  [per_device(): stacked[None]]
  transfers between devices with their start and end apart: 4 -> 3, of which waited for: 3 -> 3; matrix products, arithmetic and copies ran while one was open for 10% -> 0% of each run, Pallas kernels for 0% -> 6%
where the time goes in v1:
time: 234 us; the launch traced here: 231 us
  waiting for transfers between devices  152 us (65%)
  blocking collectives  40.4 us (17%)
  Pallas kernels  15.5 us (7%)
  between operations  13.8 us (6%)
  local copies, waits for them, and re-layouts  9.27 us (4%)
    all_gather x1, waiting for transfers between devices, per_device(): lax.all_gather(arrived.reshape(edata * flight * CAP, width), 'dp', axis=0)  79.1 us
    all_to_all x1, blocking collectives, per_device(): lax.all_to_all(outgoing.reshape(edata * flight, CAP, width), ('edata', 'e...  40.4 us
    reduce_scatter x1, waiting for transfers between devices, per_device(): lax.psum_scatter(partial, 'edata', scatter_dimension=0, tiled=False)  38.3 us
    all_gather x1, waiting for transfers between devices, per_device(): hidden = lax.all_gather(saved_hidden[0].T, 'edata', axis=0)  33.7 us
    pallas_call x1, Pallas kernels, hidden_partial(): pl.pallas_call(hidden_kernel, grid=(parts,), in_specs=[pl.BlockSpec((unit...  7.98 us
    unnamed x16, local copies, waits for them, and re-layouts  7.93 us
    pallas_call x1, Pallas kernels, weight_grad(): pl.pallas_call(weight_kernel, grid=(parts,), in_specs=[pl.BlockSpec((1, u...  5.23 us
  transfers between devices with their start and end apart: 3, of which 3 were waited for; matrix products, arithmetic and copies ran while one was open for 0% of the time, Pallas kernels for 6%

profile of v1, /device:TPU:1, one launch (start us, length us, event | category | flops | bytes accessed | tf_op | source)
XLA Modules:
  0.0 230.8 jit_solution(5005684242079025458)
XLA Ops:
  7.2 0.0 all-gather.4.cloned.1.call-start
  7.2 0.0 copy-start.2
  7.2 1.5 copy-done.2
  8.7 0.0 copy-start.4
  8.7 0.7 copy-done.4
  9.4 0.0 copy-start.5
  9.4 0.7 copy-done.5
  10.1 0.0 copy-start.6
  10.1 0.7 copy-done.6
  10.8 0.0 copy-start.7
  10.8 0.7 copy-done.7
  11.4 2.3 shard_map.86
  13.7 0.2 reshape.10
  13.9 0.0 copy-start.3
  13.9 40.4 %all_to_all.5 = bf16[128,4,896]{2,1,0:T(4,128)(2,1)S(1)} all-to-all(bf16[128,4,896]{2,1,0:T(4,128)(2,1)S(1)} %reshape.10), channel_id=1, replica_groups=mesh['dp'=4,'edata'=8,'expert'=16] {'edata','expert'}, dimensions={0} | all-to-all | bytes 1835008 | tf_op jit(solution)/shard_map/all_to_all | solution.py:124
  54.3 1.1 all_gather_reshape.3
  55.5 0.0 all-gather.4.cloned.1.call-update
  55.5 0.0 all-gather.6.cloned.1.call-start
  55.5 0.7 all-gather.6.cloned.1.call-update
  56.2 0.0 reduce-scatter.2.cloned.1.call-start
  56.3 79.1 %all-gather.4.cloned.1.call-done = bf16[4,512,896]{2,1,0:T(8,128)(2,1)} async-done(((bf16[1,512,896]{2,1,0:T(8,128)(2,1)}), bf16[4,512,896]{2,1,0:T(8,128)(2,1)}) %all-gather.4.cloned.1.call-update) | async-done | bytes 3670032 | tf_op jit(solution)/shard_map/all_gather | solution.py:131
  135.4 0.0 copy-done.3
  135.4 8.0 %shard_map.87 = bf16[8,608,256]{2,1,0:T(8,128)(2,1)} custom-call(bf16[608,896]{1,0:T(8,128)(2,1)S(1)} %bitcast.18, bf16[8,256,896]{2,1,0:T(8,128)(2,1)} %bitcast.15), custom_call_target="tpu_custom_call" | custom-call | tf_op jit(solution)/shard_map/pallas_call | solution.py:73
  143.3 0.0 reduce-scatter.2.cloned.1.call-update
  143.4 33.7 %all-gather.6.cloned.1.call-done = bf16[4864,256]{1,0:T(8,128)(2,1)} async-done(((bf16[608,256]{1,0:T(8,128)(2,1)}), bf16[4864,256]{1,0:T(8,128)(2,1)}) %all-gather.6.cloned.1.call-update) | async-done | bytes 2490384 | tf_op jit(solution)/shard_map/all_gather | solution.py:133
  177.1 0.0 copy-start
  177.1 2.0 copy-done
  179.1 0.0 copy-start.1
  179.1 1.7 copy-done.1
  180.8 5.2 %shard_map.88 = bf16[608,896]{1,0:T(8,128)(2,1)} custom-call(bf16[8,608,256]{2,1,0:T(8,128)(2,1)S(1)} %bitcast.17, bf16[8,256,896]{2,1,0:T(8,128)(2,1)S(1)} %bitcast.16), custom_call_target="tpu_custom_call" | custom-call | tf_op jit(solution)/shard_map/pallas_call | solution.py:103
  186.0 38.3 %reduce-scatter.2.cloned.1.call-done = bf16[1,608,256]{2,1,0:T(8,128)(2,1)} async-done(((bf16[8,608,256]{2,1,0:T(8,128)(2,1)}), bf16[1,608,256]{2,1,0:T(8,128)(2,1)}) %reduce-scatter.2.cloned.1.call-update) | async-done | bytes 311312 | tf_op jit(solution)/shard_map/reduce_scatter | solution.py:135
Async XLA Ops:
  7.2 128.2 %all-gather.4.cloned.1.call-start = ((), (), s32[]{:S(2)}) async-start(), calls=%async_computation.2 | async-start | bytes 4587520 | tf_op jit(solution)/shard_map/all_gather | solution.py:131
  7.2 1.5 copy-start.2
  8.7 0.7 copy-start.4
  9.4 0.7 copy-start.5
  10.1 0.7 copy-start.6
  10.8 0.7 copy-start.7
  13.9 121.5 %copy-start.3 = (bf16[1,608,896]{2,1,0:T(8,128)(2,1)S(1)}, bf16[1,608,896]{2,1,0:T(8,128)(2,1)}, u32[]{:S(2)}) copy-start(bf16[1,608,896]{2,1,0:T(8,128)(2,1)} %param.12) | copy-start | bytes 3268612
  55.5 121.6 %all-gather.6.cloned.1.call-start = ((), (), s32[]{:S(2)}) async-start(), calls=%async_computation.4 | async-start | bytes 2801664 | tf_op jit(solution)/shard_map/all_gather | solution.py:133
  56.2 168.1 %reduce-scatter.2.cloned.1.call-start = ((), (), s32[]{:S(2)}) async-start(), calls=%async_computation.3 | async-start | bytes 2801664 | tf_op jit(solution)/shard_map/reduce_scatter | solution.py:135
  177.1 2.0 copy-start
  179.1 1.7 copy-start.1
Sparse Core Ops, SparseCore 0:
  55.6 79.6 all-gather.3
  137.4 39.5 all-gather.5
  180.5 43.7 reduce-scatter.1

commit v2 on v0

v2 whole, which is shorter than its diff:
```python
import jax
import jax.numpy as jnp
from jax import lax
from jax.experimental import pallas as pl
from jax.experimental.pallas import tpu as pltpu
from jax.sharding import PartitionSpec as P

EXP_DEV = 8
CAP = 4
PARTS = 8
QUARTERS = 4
VMEM_LIMIT = 60 * 1024 * 1024


def full(count):
    return [pl.BlockSpec(memory_space=pltpu.VMEM)] * count


def lying(count):
    return [pl.BlockSpec(memory_space=pltpu.HBM)] * count


def params():
    return pltpu.CompilerParams(vmem_limit_bytes=VMEM_LIMIT)


def dispatch_kernel(prob_ref, ids_ref, slots_ref, counts_ref, grad_ref, out_ref, *scratch):
    prob_v, ids_v, slots_v, counts_v, grad_v, sems = scratch
    blocks, rows, width = out_ref.shape
    flight = counts_v.shape[1]
    tokens = grad_v.shape[1]
    copies = [
        pltpu.make_async_copy(source, place, sems.at[index])
        for index, (source, place) in enumerate(
            ((ids_ref, ids_v), (slots_ref, slots_v), (counts_ref, counts_v), (prob_ref, prob_v))
        )
    ]
    for block in range(blocks):
        copies.append(
            pltpu.make_async_copy(
                grad_ref.at[:, pl.ds(block * width, width)], grad_v.at[block], sems.at[4 + block]
            )
        )
    for copy in copies:
        copy.start()
    own = lax.broadcasted_iota(jnp.int32, (rows, flight), 0) // CAP
    column = lax.broadcasted_iota(jnp.int32, (rows, flight), 1)
    row = lax.broadcasted_iota(jnp.int32, (rows, tokens), 0)
    expert = (row // CAP) * EXP_DEV
    slot = row % CAP
    for copy in copies[:4]:
        copy.wait()
    limit = jnp.sum(jnp.where(own == column, counts_v[...], 0), axis=1, keepdims=True)
    picker = jnp.zeros((rows, tokens), jnp.float32)
    scale = jnp.zeros((rows, 1), jnp.float32)
    for choice in range(2):
        match = (
            (ids_v[choice : choice + 1, :] == expert)
            & (slots_v[choice : choice + 1, :] == slot)
            & (slot < limit)
        )
        picker = picker + jnp.where(match, 1.0, 0.0)
        scale = scale + jnp.sum(
            jnp.where(match, prob_v[choice : choice + 1, :], 0.0), axis=1, keepdims=True
        )
    picker = picker.astype(jnp.bfloat16)
    for block in range(blocks):
        copies[4 + block].wait()
        picked = jnp.dot(picker, grad_v[block], preferred_element_type=jnp.float32)
        out_ref[block] = (picked * scale).astype(out_ref.dtype)


def dispatch(route_prob, expert_ids, slots, counts, out_grad, blocks):
    tokens, model = out_grad.shape
    flight = counts.shape[1]
    width = model // blocks
    return pl.pallas_call(
        dispatch_kernel,
        in_specs=lying(5),
        out_specs=full(1)[0],
        out_shape=jax.ShapeDtypeStruct((blocks, flight * CAP, width), jnp.bfloat16),
        scratch_shapes=[
            pltpu.VMEM((2, tokens), jnp.float32),
            pltpu.VMEM((2, tokens), jnp.int32),
            pltpu.VMEM((2, tokens), jnp.int32),
            pltpu.VMEM((1, flight), jnp.int32),
            pltpu.VMEM((blocks, tokens, width), jnp.bfloat16),
            pltpu.SemaphoreType.DMA((4 + blocks,)),
        ],
        compiler_params=params(),
    )(route_prob.T, expert_ids.T, slots.T, counts, out_grad)


def turn_kernel(weight_ref, out_ref):
    out_ref[...] = weight_ref[...].T


def turn(weight):
    units, width = weight.shape
    return pl.pallas_call(
        turn_kernel,
        in_specs=full(1),
        out_specs=full(1)[0],
        out_shape=jax.ShapeDtypeStruct((width, units), weight.dtype),
        compiler_params=params(),
    )(weight)


def hidden_kernel(weight_ref, *refs):
    count = len(refs) - 6
    pieces = refs[:count]
    out_ref, weight_v, rows_v, result_v, sems, out_sems = refs[count:]
    _, parts, slots, units = result_v.shape
    load = pltpu.make_async_copy(weight_ref, weight_v, sems.at[count])
    load.start()
    copies = [
        pltpu.make_async_copy(piece, rows_v.at[index], sems.at[index])
        for index, piece in enumerate(pieces)
    ]
    for copy in copies:
        copy.start()
    load.wait()
    stores = []
    for index in range(count):
        copies[index].wait()
        product = jnp.dot(rows_v[index], weight_v[...], preferred_element_type=jnp.float32)
        result_v[index] = product.astype(result_v.dtype).reshape(parts, slots, units)
        stores.append(
            pltpu.make_async_copy(
                result_v.at[index], out_ref.at[:, pl.ds(index * slots, slots)], out_sems.at[index]
            )
        )
        stores[-1].start()
    for store in stores:
        store.wait()


def hidden_partial(weight, pieces):
    width, units = weight.shape
    rows = pieces[0].shape[0]
    count = len(pieces)
    slots = rows // PARTS
    return pl.pallas_call(
        hidden_kernel,
        in_specs=lying(1 + count),
        out_specs=lying(1)[0],
        out_shape=jax.ShapeDtypeStruct((PARTS, count * slots, units), jnp.bfloat16),
        scratch_shapes=[
            pltpu.VMEM((width, units), jnp.bfloat16),
            pltpu.VMEM((count, rows, width), jnp.bfloat16),
            pltpu.VMEM((count, PARTS, slots, units), jnp.bfloat16),
            pltpu.SemaphoreType.DMA((count + 1,)),
            pltpu.SemaphoreType.DMA((count,)),
        ],
        compiler_params=params(),
    )(weight, *pieces)


def weight_kernel(hidden_ref, *refs):
    pieces = refs[:-4]
    out_ref, rows_v, hidden_v, sems = refs[-4:]
    parts, _, size = hidden_ref.shape
    slots = size // len(pieces)
    copies = []
    for part in range(parts):
        copies.append(
            pltpu.make_async_copy(
                hidden_ref.at[part], hidden_v.at[:, pl.ds(part * size, size)], sems.at[0, part]
            )
        )
        for index, piece in enumerate(pieces):
            copies.append(
                pltpu.make_async_copy(
                    piece.at[pl.ds(part * slots, slots)],
                    rows_v.at[pl.ds(part * size + index * slots, slots)],
                    sems.at[1 + index, part],
                )
            )
    for copy in copies:
        copy.start()
    for copy in copies:
        copy.wait()
    out_ref[...] = jnp.dot(
        hidden_v[...], rows_v[...], preferred_element_type=jnp.float32
    ).astype(out_ref.dtype)


def weight_grad(hidden, pieces):
    parts, units, size = hidden.shape
    width = pieces[0].shape[1]
    return pl.pallas_call(
        weight_kernel,
        in_specs=lying(1 + len(pieces)),
        out_specs=full(1)[0],
        out_shape=jax.ShapeDtypeStruct((units, width), jnp.bfloat16),
        scratch_shapes=[
            pltpu.VMEM((parts * size, width), jnp.bfloat16),
            pltpu.VMEM((units, parts * size), jnp.bfloat16),
            pltpu.SemaphoreType.DMA((1 + len(pieces), parts)),
        ],
        compiler_params=params(),
    )(hidden, *pieces)


def finish_kernel(sums_ref, last_ref, out_ref):
    last = jnp.sum(last_ref[...].astype(jnp.float32), axis=0).astype(jnp.bfloat16)
    joined = jnp.concatenate([sums_ref[...], last], axis=0)
    size = joined.shape[0]
    first = lax.broadcasted_iota(jnp.int32, (size, size), 0)
    second = lax.broadcasted_iota(jnp.int32, (size, size), 1)
    same = jnp.where(first == second, 1.0, 0.0).astype(jnp.bfloat16)
    out_ref[...] = lax.dot_general(
        joined, same, (((0,), (0,)), ((), ())), preferred_element_type=jnp.float32
    ).astype(out_ref.dtype)


def finish(sums, last):
    slots, units = sums.shape
    return pl.pallas_call(
        finish_kernel,
        in_specs=full(2),
        out_specs=full(1)[0],
        out_shape=jax.ShapeDtypeStruct((units, slots + last.shape[1]), jnp.bfloat16),
        compiler_params=params(),
    )(sums, last)


def per_device(out_grad, route_prob, expert_ids, slots, counts, down_weight, saved_hidden):
    flight = lax.axis_size("expert")
    edata = lax.axis_size("edata")
    width = out_grad.shape[1] // edata
    outgoing = dispatch(route_prob, expert_ids, slots, counts, out_grad, edata)
    arrived = lax.all_to_all(
        outgoing.reshape(edata * flight, CAP, width),
        ("edata", "expert"),
        split_axis=0,
        concat_axis=0,
        tiled=True,
    )
    arrived, hidden, weight = lax.optimization_barrier(
        (arrived, saved_hidden[0].T, turn(down_weight[0]))
    )
    hidden = lax.all_gather(hidden, "edata", axis=0)
    blocks = arrived.reshape(2, QUARTERS, -1, width)
    quarters = [blocks[:, index].reshape(-1, width) for index in range(QUARTERS)]
    gathered = [lax.all_gather(quarter, "dp", axis=0, tiled=True) for quarter in quarters[:2]]
    third, hidden = lax.optimization_barrier((quarters[2], hidden))
    gathered.append(lax.all_gather(third, "dp", axis=0, tiled=True))
    partial = hidden_partial(weight, gathered)
    partial, fourth = lax.optimization_barrier((partial, quarters[3]))
    sums = lax.psum_scatter(partial, "edata", scatter_dimension=0, tiled=False)
    gathered.append(lax.all_gather(fourth, "dp", axis=0, tiled=True))
    spread = lax.all_to_all(
        hidden_partial(weight, gathered[3:]), "edata", split_axis=0, concat_axis=0, tiled=True
    )
    grad = weight_grad(hidden, gathered)
    return finish(sums, spread).T[None], grad[None]


def solution(mesh):
    placed = (
        P(("dp", "edata", "expert"), None),
        P(("dp", "edata", "expert"), None),
        P(("dp", "edata", "expert"), None),
        P(("dp", "edata", "expert"), None),
        P(("dp", "edata", "expert"), None),
        P("expert", "dp", "edata"),
        P("expert", "edata", "dp"),
    )
    return jax.shard_map(
        per_device,
        mesh=mesh,
        in_specs=placed,
        out_specs=(P("expert", "edata", "dp"), P("expert", "dp", "edata")),
        check_vma=False,
    )
```

time: 331 us -> 186 us (0.56)
  the two profiles are of different devices: /device:TPU:1 before, /device:TPU:8 now
where the time goes in v2:
time: 186 us
  blocking collectives  87.7 us (47%)
  waiting for transfers between devices  39.4 us (21%)
  Pallas kernels  24.2 us (13%)
  starting transfers between devices  17 us (9%)
  between operations  14.1 us (8%)
  local copies, waits for them, and re-layouts  3.65 us (2%)
    all_gather x2, blocking collectives, per_device(): lax.all_gather(quarter, 'dp', axis=0, tiled=True)  49.8 us
    all_to_all x1, waiting for transfers between devices, per_device(): lax.all_to_all(outgoing.reshape(edata * flight, CAP, width), ('edata', 'e...  24 us
    all_gather x1, blocking collectives, per_device(): gathered.append(lax.all_gather(third, 'dp', axis=0, tiled=True))  20.1 us
    all_gather x1, blocking collectives, per_device(): gathered.append(lax.all_gather(fourth, 'dp', axis=0, tiled=True))  17.9 us
    all_to_all x1, waiting for transfers between devices, per_device(): lax.all_to_all(hidden_partial(weight, gathered[3:]), 'edata', split_axis=...  15.4 us
    all_to_all x1, starting transfers between devices, per_device(): lax.all_to_all(outgoing.reshape(edata * flight, CAP, width), ('edata', 'e...  13.2 us
    pallas_call x2, Pallas kernels, hidden_partial(): pl.pallas_call(hidden_kernel, in_specs=lying(1 + count), out_specs=lying(...  8.99 us
    pallas_call x1, Pallas kernels, weight_grad(): pl.pallas_call(weight_kernel, in_specs=lying(1 + len(pieces)), out_specs=...  6.85 us
  transfers between devices with their start and end apart: 4, of which 2 were waited for; matrix products, arithmetic and copies ran while one was open for 0% of the time, Pallas kernels for 7%

profile of v2, /device:TPU:8, one launch (start us, length us, event | category | flops | bytes accessed | tf_op | source)
XLA Modules:
  0.0 186.0 jit_solution(2382788504006771957)
XLA Ops:
  7.2 3.4 %shard_map.86 = bf16[8,64,896]{2,1,0:T(8,128)(2,1)} custom-call(f32[2,128]{1,0:T(2,128)} %bitcast.27, s32[2,128]{1,0:T(2,128)} %bitcast.28, s32[2,128]{1,0:T(2,128)} %bitcast.29, s32[1,16]{1,0:T(1,128)} %counts_ref.1, bf16[128,7168]{1,0:T(8,128)(2,1)} %grad_ref.1), custom_call_target="tpu_custom_call" | custom-call | tf_op jit(solution)/shard_map/pallas_call | solution.py:77
  10.6 2.5 %reshape.10 = bf16[128,4,896]{2,1,0:T(4,128)(2,1)} reshape(bf16[8,64,896]{2,1,0:T(8,128)(2,1)} %shard_map.86) | data formatting | bytes 1835008 | tf_op jit(solution)/shard_map/reshape | solution.py:234
  13.1 13.2 %all-to-all-start = ((bf16[128,4,896]{2,1,0:T(4,128)(2,1)}), bf16[128,4,896]{2,1,0:T(4,128)(2,1)S(1)}, u32[]{:S(2)}, u32[]{:S(2)}) async-start(bf16[128,4,896]{2,1,0:T(4,128)(2,1)} %reshape.10), calls=%async_computation | async-start | bytes 1835008 | tf_op jit(solution)/shard_map/all_to_all | solution.py:233
  26.3 0.0 all-gather.3.cloned.1.call-start
  26.4 2.6 %shard_map.87.weight_ref = bf16[896,608]{1,0:T(8,128)(2,1)} custom-call(bf16[608,896]{1,0:T(8,128)(2,1)} %bitcast.18), custom_call_target="tpu_custom_call" | custom-call | tf_op jit(solution)/shard_map/pallas_call | solution.py:100
  29.0 24.0 %all-to-all-done = bf16[128,4,896]{2,1,0:T(4,128)(2,1)S(1)} async-done(((bf16[128,4,896]{2,1,0:T(4,128)(2,1)}), bf16[128,4,896]{2,1,0:T(4,128)(2,1)S(1)}, u32[]{:S(2)}, u32[]{:S(2)}) %all-to-all-start) | async-done | bytes 917536 | tf_op jit(solution)/shard_map/all_to_all | solution.py:233
  53.0 0.0 all-gather.3.cloned.1.call-update
  53.0 0.0 reduce-scatter.2.cloned.1.call-start
  53.1 0.2 reshape.11
  53.3 0.1 fusion
  53.4 27.4 %all_gather.19.refs_1_ = bf16[512,896]{1,0:T(8,128)(2,1)} all-gather(bf16[128,896]{1,0:T(8,128)(2,1)S(1)} %bitcast.23), channel_id=1, replica_groups=mesh['dp'=4,'edata'=8,'expert'=16] {'dp'}, dimensions={0}, use_global_device_ids=true | all-gather | bytes 1146880 | tf_op jit(solution)/shard_map/all_gather | solution.py:246
  80.8 22.4 %all_gather.18.refs_0_ = bf16[512,896]{1,0:T(8,128)(2,1)} all-gather(bf16[128,896]{1,0:T(8,128)(2,1)S(1)} %bitcast.22), channel_id=1, replica_groups=mesh['dp'=4,'edata'=8,'expert'=16] {'dp'}, dimensions={0}, use_global_device_ids=true | all-gather | bytes 1146880 | tf_op jit(solution)/shard_map/all_gather | solution.py:246
  103.2 0.0 all-gather.3.cloned.1.call-done
  103.2 20.1 %all_gather.22.refs_2_ = bf16[512,896]{1,0:T(8,128)(2,1)} all-gather(bf16[128,896]{1,0:T(8,128)(2,1)S(1)} %bitcast.21), channel_id=1, replica_groups=mesh['dp'=4,'edata'=8,'expert'=16] {'dp'}, dimensions={0}, use_global_device_ids=true | all-gather | bytes 1146880 | tf_op jit(solution)/shard_map/all_gather | solution.py:248
  123.2 5.7 %shard_map.88 = bf16[8,192,608]{2,1,0:T(8,128)(2,1)} custom-call(bf16[896,608]{1,0:T(8,128)(2,1)} %shard_map.87.weight_ref, bf16[512,896]{1,0:T(8,128)(2,1)} %all_gather.18.refs_0_, bf16[512,896]{1,0:T(8,128)(2,1)} %all_gather.19.refs_1_, bf16[512,896]{1,0:T(8,128)(2,1)} %all_gather.22.refs_2_), custom_call_target="tpu_custom_call" | custom-call | tf_op jit(solution)/shard_map/pallas_call | solution.py:143
  128.9 0.0 reduce-scatter.2.cloned.1.call-update
  128.9 17.9 %all_gather.23.refs_0_.refs_3_ = bf16[512,896]{1,0:T(8,128)(2,1)} all-gather(bf16[128,896]{1,0:T(8,128)(2,1)S(1)} %bitcast.20), channel_id=1, replica_groups=mesh['dp'=4,'edata'=8,'expert'=16] {'dp'}, dimensions={0}, use_global_device_ids=true | all-gather | bytes 1146880 | tf_op jit(solution)/shard_map/all_gather | solution.py:252
  146.8 3.3 %shard_map.89 = bf16[8,64,608]{2,1,0:T(8,128)(2,1)} custom-call(bf16[896,608]{1,0:T(8,128)(2,1)} %shard_map.87.weight_ref, bf16[512,896]{1,0:T(8,128)(2,1)} %all_gather.23.refs_0_.refs_3_), custom_call_target="tpu_custom_call" | custom-call | tf_op jit(solution)/shard_map/pallas_call | solution.py:143
  150.1 3.7 %all-to-all-start.1 = ((bf16[8,64,608]{2,1,0:T(8,128)(2,1)}), bf16[8,64,608]{2,1,0:T(8,128)(2,1)S(1)}, u32[]{:S(2)}, u32[]{:S(2)}) async-start(bf16[8,64,608]{2,1,0:T(8,128)(2,1)} %shard_map.89), calls=%async_computation.2 | async-start | bytes 1310720 | tf_op jit(solution)/shard_map/all_to_all | solution.py:253
  153.9 6.9 %shard_map.91 = bf16[608,896]{1,0:T(8,128)(2,1)} custom-call(bf16[8,608,256]{2,1,0:T(8,128)(2,1)} %bitcast.17, bf16[512,896]{1,0:T(8,128)(2,1)} %all_gather.18.refs_0_, bf16[512,896]{1,0:T(8,128)(2,1)} %all_gather.19.refs_1_, bf16[512,896]{1,0:T(8,128)(2,1)} %all_gather.22.refs_2_, bf16[512,896]{1,0:T(8,128)(2,1)} %all_gather.23.refs_0_.refs_3_), custom_call_target="tpu_custom_call" | custom-call | tf_op jit(solution)/shard_map/pallas_call | solution.py:191
  160.7 15.4 %all-to-all-done.1.last_ref = bf16[8,64,608]{2,1,0:T(8,128)(2,1)S(1)} async-done(((bf16[8,64,608]{2,1,0:T(8,128)(2,1)}), bf16[8,64,608]{2,1,0:T(8,128)(2,1)S(1)}, u32[]{:S(2)}, u32[]{:S(2)}) %all-to-all-start.1) | async-done | bytes 622624 | tf_op jit(solution)/shard_map/all_to_all | solution.py:253
  176.1 0.0 copy-start
  176.1 0.0 reduce-scatter.2.cloned.1.call-done
  176.1 0.8 copy-done
  176.9 2.3 %shard_map.90 = bf16[608,256]{1,0:T(8,128)(2,1)} custom-call(bf16[192,608]{1,0:T(8,128)(2,1)} %bitcast.26, bf16[8,64,608]{2,1,0:T(8,128)(2,1)} %copy-done), custom_call_target="tpu_custom_call" | custom-call | tf_op jit(solution)/shard_map/pallas_call | solution.py:219
Async XLA Ops:
  13.1 39.8 %all-to-all-start = ((bf16[128,4,896]{2,1,0:T(4,128)(2,1)}), bf16[128,4,896]{2,1,0:T(4,128)(2,1)S(1)}, u32[]{:S(2)}, u32[]{:S(2)}) async-start(bf16[128,4,896]{2,1,0:T(4,128)(2,1)} %reshape.10), calls=%async_computation | async-start | bytes 1835008 | tf_op jit(solution)/shard_map/all_to_all | solution.py:233
  26.3 76.8 %all-gather.3.cloned.1.call-start = ((), (), s32[]{:S(2)}) async-start(), calls=%async_computation.4 | async-start | bytes 2801664 | tf_op jit(solution)/shard_map/all_gather | solution.py:243
  53.0 123.1 %reduce-scatter.2.cloned.1.call-start = ((), (), s32[]{:S(2)}) async-start(), calls=%async_computation.3 | async-start | bytes 2211840 | tf_op jit(solution)/shard_map/reduce_scatter | solution.py:251
  150.1 26.0 %all-to-all-start.1 = ((bf16[8,64,608]{2,1,0:T(8,128)(2,1)}), bf16[8,64,608]{2,1,0:T(8,128)(2,1)S(1)}, u32[]{:S(2)}, u32[]{:S(2)}) async-start(bf16[8,64,608]{2,1,0:T(8,128)(2,1)} %shard_map.89), calls=%async_computation.2 | async-start | bytes 1310720 | tf_op jit(solution)/shard_map/all_to_all | solution.py:253
  176.1 0.8 copy-start
Sparse Core Ops, SparseCore 0:
  53.1 42.8 all-gather.2
  129.0 45.2 reduce-scatter.1

commit v3 on v2

--- a/solution.py
+++ b/solution.py
@@ -17,7 +17,11 @@
 
 
 def lying(count):
-    return [pl.BlockSpec(memory_space=pltpu.HBM)] * count
+    return [pl.BlockSpec(memory_space=pl.ANY)] * count
+
+
+def scalar():
+    return [pl.BlockSpec(memory_space=pltpu.SMEM)]
 
 
 def params():
@@ -26,8 +30,10 @@
 
 def dispatch_kernel(prob_ref, ids_ref, slots_ref, counts_ref, grad_ref, out_ref, *scratch):
     prob_v, ids_v, slots_v, counts_v, grad_v, sems = scratch
-    blocks, rows, width = out_ref.shape
+    width = out_ref.shape[2]
     flight = counts_v.shape[1]
+    rows = flight * CAP
+    blocks = out_ref.shape[0] // flight
     tokens = grad_v.shape[1]
     copies = [
         pltpu.make_async_copy(source, place, sems.at[index])
@@ -67,7 +73,9 @@
     for block in range(blocks):
         copies[4 + block].wait()
         picked = jnp.dot(picker, grad_v[block], preferred_element_type=jnp.float32)
-        out_ref[block] = (picked * scale).astype(out_ref.dtype)
+        out_ref[block * flight : (block + 1) * flight] = (
+            (picked * scale).reshape(flight, CAP, width).astype(out_ref.dtype)
+        )
 
 
 def dispatch(route_prob, expert_ids, slots, counts, out_grad, blocks):
@@ -78,7 +86,7 @@
         dispatch_kernel,
         in_specs=lying(5),
         out_specs=full(1)[0],
-        out_shape=jax.ShapeDtypeStruct((blocks, flight * CAP, width), jnp.bfloat16),
+        out_shape=jax.ShapeDtypeStruct((blocks * flight, CAP, width), jnp.bfloat16),
         scratch_shapes=[
             pltpu.VMEM((2, tokens), jnp.float32),
             pltpu.VMEM((2, tokens), jnp.int32),
@@ -106,28 +114,39 @@
     )(weight)
 
 
-def hidden_kernel(weight_ref, *refs):
-    count = len(refs) - 6
-    pieces = refs[:count]
-    out_ref, weight_v, rows_v, result_v, sems, out_sems = refs[count:]
-    _, parts, slots, units = result_v.shape
-    load = pltpu.make_async_copy(weight_ref, weight_v, sems.at[count])
+def place_of(place, shift):
+    return lax.rem(place + shift, PARTS // 2) * 2
+
+
+def near_kernel(place_ref, weight_ref, *refs):
+    pieces = refs[:6]
+    out_ref, weight_v, near_v, near_out, sems, out_sems = refs[6:]
+    _, half, units = out_ref.shape
+    load = pltpu.make_async_copy(weight_ref, weight_v, sems.at[6])
     load.start()
     copies = [
-        pltpu.make_async_copy(piece, rows_v.at[index], sems.at[index])
+        pltpu.make_async_copy(
+            piece, near_v.at[index // 2, pl.ds(index % 2 * half, half)], sems.at[index]
+        )
         for index, piece in enumerate(pieces)
     ]
     for copy in copies:
         copy.start()
     load.wait()
     stores = []
-    for index in range(count):
-        copies[index].wait()
-        product = jnp.dot(rows_v[index], weight_v[...], preferred_element_type=jnp.float32)
-        result_v[index] = product.astype(result_v.dtype).reshape(parts, slots, units)
+    for index, shift in enumerate((0, 3, 1)):
+        copies[2 * index].wait()
+        copies[2 * index + 1].wait()
+        near_out[index] = (
+            jnp.dot(near_v[index], weight_v[...], preferred_element_type=jnp.float32)
+            .astype(near_out.dtype)
+            .reshape(2, half, units)
+        )
         stores.append(
             pltpu.make_async_copy(
-                result_v.at[index], out_ref.at[:, pl.ds(index * slots, slots)], out_sems.at[index]
+                near_out.at[index],
+                out_ref.at[pl.ds(place_of(place_ref[0], shift), 2)],
+                out_sems.at[index],
             )
         )
         stores[-1].start()
@@ -135,33 +154,104 @@
         store.wait()
 
 
-def hidden_partial(weight, pieces):
+def near_partial(place, weight, near):
     width, units = weight.shape
-    rows = pieces[0].shape[0]
-    count = len(pieces)
-    slots = rows // PARTS
-    return pl.pallas_call(
-        hidden_kernel,
-        in_specs=lying(1 + count),
+    half = near[0].shape[0]
+    return pl.pallas_call(
+        near_kernel,
+        in_specs=scalar() + lying(7),
         out_specs=lying(1)[0],
-        out_shape=jax.ShapeDtypeStruct((PARTS, count * slots, units), jnp.bfloat16),
+        out_shape=jax.ShapeDtypeStruct((PARTS, half, units), jnp.bfloat16),
         scratch_shapes=[
             pltpu.VMEM((width, units), jnp.bfloat16),
-            pltpu.VMEM((count, rows, width), jnp.bfloat16),
-            pltpu.VMEM((count, PARTS, slots, units), jnp.bfloat16),
-            pltpu.SemaphoreType.DMA((count + 1,)),
-            pltpu.SemaphoreType.DMA((count,)),
+            pltpu.VMEM((3, 2 * half, width), jnp.bfloat16),
+            pltpu.VMEM((3, 2, half, units), jnp.bfloat16),
+            pltpu.SemaphoreType.DMA((7,)),
+            pltpu.SemaphoreType.DMA((3,)),
         ],
         compiler_params=params(),
-    )(weight, *pieces)
-
-
-def weight_kernel(hidden_ref, *refs):
-    pieces = refs[:-4]
+    )(place, weight, *near)
+
+
+def far_kernel(place_ref, weight_ref, first_ref, second_ref, _, out_ref, *scratch):
+    weight_v, far_v, far_out, sems = scratch
+    half, units = far_out.shape[1:]
+    copies = [
+        pltpu.make_async_copy(weight_ref, weight_v, sems.at[0]),
+        pltpu.make_async_copy(first_ref, far_v.at[pl.ds(0, half)], sems.at[1]),
+        pltpu.make_async_copy(second_ref, far_v.at[pl.ds(half, half)], sems.at[2]),
+    ]
+    for copy in copies:
+        copy.start()
+    for copy in copies:
+        copy.wait()
+    far_out[...] = (
+        jnp.dot(far_v[...], weight_v[...], preferred_element_type=jnp.float32)
+        .astype(far_out.dtype)
+        .reshape(2, half, units)
+    )
+    store = pltpu.make_async_copy(
+        far_out, out_ref.at[pl.ds(place_of(place_ref[0], 2), 2)], sems.at[3]
+    )
+    store.start()
+    store.wait()
+
+
+def far_partial(place, weight, far, partial):
+    width, units = weight.shape
+    half = far[0].shape[0]
+    return pl.pallas_call(
+        far_kernel,
+        in_specs=scalar() + lying(4),
+        out_specs=lying(1)[0],
+        out_shape=jax.ShapeDtypeStruct(partial.shape, partial.dtype),
+        scratch_shapes=[
+            pltpu.VMEM((width, units), jnp.bfloat16),
+            pltpu.VMEM((2 * half, width), jnp.bfloat16),
+            pltpu.VMEM((2, half, units), jnp.bfloat16),
+            pltpu.SemaphoreType.DMA((4,)),
+        ],
+        input_output_aliases={4: 0},
+        compiler_params=params(),
+    )(place, weight, *far, partial)
+
+
+def last_kernel(weight_ref, rows_ref, out_ref):
+    out_ref[...] = (
+        jnp.dot(rows_ref[...], weight_ref[...], preferred_element_type=jnp.float32)
+        .astype(out_ref.dtype)
+        .reshape(out_ref.shape)
+    )
+
+
+def last_partial(weight, rows):
+    return pl.pallas_call(
+        last_kernel,
+        in_specs=full(2),
+        out_specs=full(1)[0],
+        out_shape=jax.ShapeDtypeStruct(
+            (PARTS, rows.shape[0] // PARTS, weight.shape[1]), jnp.bfloat16
+        ),
+        compiler_params=params(),
+    )(weight, rows)
+
+
+def weight_kernel(place_ref, hidden_ref, *refs):
+    near, pieces = refs[:8], refs[8:-4]
     out_ref, rows_v, hidden_v, sems = refs[-4:]
     parts, _, size = hidden_ref.shape
-    slots = size // len(pieces)
+    half = near[0].shape[0]
+    slots = (size - half) // len(pieces)
     copies = []
+
+    def fetch(piece, target, start, count, number):
+        row = pl.multiple_of(target * size + start, slots)
+        copies.append(
+            pltpu.make_async_copy(
+                piece, rows_v.at[pl.ds(row, count)], sems.at[number // parts, number % parts]
+            )
+        )
+
     for part in range(parts):
         copies.append(
             pltpu.make_async_copy(
@@ -169,13 +259,16 @@
             )
         )
         for index, piece in enumerate(pieces):
-            copies.append(
-                pltpu.make_async_copy(
-                    piece.at[pl.ds(part * slots, slots)],
-                    rows_v.at[pl.ds(part * size + index * slots, slots)],
-                    sems.at[1 + index, part],
-                )
-            )
+            fetch(
+                piece.at[pl.ds(part * slots, slots)],
+                part,
+                half + index * slots,
+                slots,
+                parts * (1 + index) + part,
+            )
+    for index, piece in enumerate(near):
+        target = place_of(place_ref[0], (0, 3, 1, 2)[index // 2]) + index % 2
+        fetch(piece, target, 0, half, parts * (1 + len(pieces)) + index)
     for copy in copies:
         copy.start()
     for copy in copies:
@@ -185,21 +278,21 @@
     ).astype(out_ref.dtype)
 
 
-def weight_grad(hidden, pieces):
+def weight_grad(place, hidden, near, far, pieces):
     parts, units, size = hidden.shape
     width = pieces[0].shape[1]
     return pl.pallas_call(
         weight_kernel,
-        in_specs=lying(1 + len(pieces)),
+        in_specs=scalar() + lying(9 + len(pieces)),
         out_specs=full(1)[0],
         out_shape=jax.ShapeDtypeStruct((units, width), jnp.bfloat16),
         scratch_shapes=[
             pltpu.VMEM((parts * size, width), jnp.bfloat16),
             pltpu.VMEM((units, parts * size), jnp.bfloat16),
-            pltpu.SemaphoreType.DMA((1 + len(pieces), parts)),
+            pltpu.SemaphoreType.DMA((2 + len(pieces), parts)),
         ],
         compiler_params=params(),
-    )(hidden, *pieces)
+    )(place, hidden, *near, *far, *pieces)
 
 
 def finish_kernel(sums_ref, last_ref, out_ref):
@@ -225,13 +318,19 @@
     )(sums, last)
 
 
+def shifted(value, axis, step):
+    size = lax.axis_size(axis)
+    return lax.ppermute(value, axis, [(i, (i + step) % size) for i in range(size)])
+
+
 def per_device(out_grad, route_prob, expert_ids, slots, counts, down_weight, saved_hidden):
     flight = lax.axis_size("expert")
     edata = lax.axis_size("edata")
     width = out_grad.shape[1] // edata
+    place = lax.axis_index("dp").astype(jnp.int32)[None]
     outgoing = dispatch(route_prob, expert_ids, slots, counts, out_grad, edata)
     arrived = lax.all_to_all(
-        outgoing.reshape(edata * flight, CAP, width),
+        outgoing,
         ("edata", "expert"),
         split_axis=0,
         concat_axis=0,
@@ -242,18 +341,24 @@
     )
     hidden = lax.all_gather(hidden, "edata", axis=0)
     blocks = arrived.reshape(2, QUARTERS, -1, width)
-    quarters = [blocks[:, index].reshape(-1, width) for index in range(QUARTERS)]
-    gathered = [lax.all_gather(quarter, "dp", axis=0, tiled=True) for quarter in quarters[:2]]
-    third, hidden = lax.optimization_barrier((quarters[2], hidden))
-    gathered.append(lax.all_gather(third, "dp", axis=0, tiled=True))
-    partial = hidden_partial(weight, gathered)
-    partial, fourth = lax.optimization_barrier((partial, quarters[3]))
+    first = blocks[0, :3].reshape(-1, width)
+    second = blocks[1, :3].reshape(-1, width)
+    fourth = blocks[:, 3].reshape(-1, width)
+    low_first = shifted(first, "dp", 1)
+    high_second = shifted(second, "dp", -1)
+    low_second = shifted(second, "dp", 1)
+    high_first = shifted(first, "dp", -1)
+    far = (shifted(low_first, "dp", 1), shifted(high_second, "dp", -1))
+    near = (first, second, low_first, low_second, high_first, high_second)
+    partial = near_partial(place, weight, near)
+    partial = far_partial(place, weight, far, partial)
+    partial, fourth, hidden = lax.optimization_barrier((partial, fourth, hidden))
     sums = lax.psum_scatter(partial, "edata", scatter_dimension=0, tiled=False)
-    gathered.append(lax.all_gather(fourth, "dp", axis=0, tiled=True))
+    fourth = lax.all_gather(fourth, "dp", axis=0, tiled=True)
     spread = lax.all_to_all(
-        hidden_partial(weight, gathered[3:]), "edata", split_axis=0, concat_axis=0, tiled=True
-    )
-    grad = weight_grad(hidden, gathered)
+        last_partial(weight, fourth), "edata", split_axis=0, concat_axis=0, tiled=True
+    )
+    grad = weight_grad(place, hidden, near, far, (fourth,))
     return finish(sums, spread).T[None], grad[None]
 
 

time: 186 us -> 173 us (0.930)
  the two profiles are of different devices: /device:TPU:8 before, /device:TPU:1 now
where the time goes in v3:
time: 173 us
  waiting for transfers between devices  51.3 us (30%)
  starting transfers between devices  48.7 us (28%)
  blocking collectives  29 us (17%)
  Pallas kernels  26.4 us (15%)
  between operations  14.3 us (8%)
  local copies, waits for them, and re-layouts  2.77 us (2%)
    all_gather x1, blocking collectives, per_device(): fourth = lax.all_gather(fourth, 'dp', axis=0, tiled=True)  29 us
    ppermute x6, starting transfers between devices, shifted(): lax.ppermute(value, axis, [(i, (i + step) % size) for i in range(size)])  25.8 us
    all_to_all x1, waiting for transfers between devices, per_device(): lax.all_to_all(outgoing, ('edata', 'expert'), split_axis=0, concat_axis=0...  23.6 us
    all_to_all x1, waiting for transfers between devices, per_device(): lax.all_to_all(last_partial(weight, fourth), 'edata', split_axis=0, conca...  15.7 us
    all_to_all x1, starting transfers between devices, per_device(): lax.all_to_all(outgoing, ('edata', 'expert'), split_axis=0, concat_axis=0...  14.2 us
    ppermute x6, waiting for transfers between devices, shifted(): lax.ppermute(value, axis, [(i, (i + step) % size) for i in range(size)])  12 us
    all_to_all x1, starting transfers between devices, per_device(): lax.all_to_all(last_partial(weight, fourth), 'edata', split_axis=0, conca...  8.64 us
    pallas_call x1, Pallas kernels, weight_grad(): pl.pallas_call(weight_kernel, in_specs=scalar() + lying(9 + len(pieces)),...  6.77 us
  transfers between devices with their start and end apart: 10, of which 5 were waited for; matrix products, arithmetic and copies ran while one was open for 0% of the time, Pallas kernels for 12%

profile of v3, /device:TPU:1, one launch (start us, length us, event | category | flops | bytes accessed | tf_op | source)
XLA Modules:
  0.0 172.5 jit_solution(15685086386288104769)
XLA Ops:
  7.2 3.5 %shard_map.86 = bf16[128,4,896]{2,1,0:T(4,128)(2,1)} custom-call(f32[2,128]{1,0:T(2,128)} %bitcast.34, s32[2,128]{1,0:T(2,128)} %bitcast.35, s32[2,128]{1,0:T(2,128)} %bitcast.36, s32[1,16]{1,0:T(1,128)} %counts_ref.1, bf16[128,7168]{1,0:T(8,128)(2,1)} %grad_ref.1), custom_call_target="tpu_custom_call" | custom-call | tf_op jit(solution)/shard_map/pallas_call | solution.py:85
  10.7 14.2 %all-to-all-start = ((bf16[128,4,896]{2,1,0:T(4,128)(2,1)}), bf16[128,4,896]{2,1,0:T(4,128)(2,1)S(1)}, u32[]{:S(2)}, u32[]{:S(2)}) async-start(bf16[128,4,896]{2,1,0:T(4,128)(2,1)} %shard_map.86), calls=%async_computation | async-start | bytes 1835008 | tf_op jit(solution)/shard_map/all_to_all | solution.py:332
  24.9 0.0 all-gather.3.cloned.1.call-start
  25.0 2.7 %shard_map.87.weight_ref = bf16[896,608]{1,0:T(8,128)(2,1)} custom-call(bf16[608,896]{1,0:T(8,128)(2,1)} %bitcast.29), custom_call_target="tpu_custom_call" | custom-call | tf_op jit(solution)/shard_map/pallas_call | solution.py:108
  27.7 23.6 %all-to-all-done = bf16[128,4,896]{2,1,0:T(4,128)(2,1)S(1)} async-done(((bf16[128,4,896]{2,1,0:T(4,128)(2,1)}), bf16[128,4,896]{2,1,0:T(4,128)(2,1)S(1)}, u32[]{:S(2)}, u32[]{:S(2)}) %all-to-all-start) | async-done | bytes 917536 | tf_op jit(solution)/shard_map/all_to_all | solution.py:332
  51.2 0.0 all-gather.3.cloned.1.call-update
  51.3 0.0 reduce-scatter.2.cloned.1.call-start
  51.3 0.2 reshape.7
  51.5 0.0 copy-start
  51.6 0.1 fusion
  51.6 0.0 copy-start.1
  51.6 0.0 copy-start.2
  51.6 5.8 %collective-permute-start = (bf16[192,896]{1,0:T(8,128)(2,1)S(1)}, bf16[192,896]{1,0:T(8,128)(2,1)S(1)}, u32[]{:S(2)}, u32[]{:S(2)}) collective-permute-start(bf16[192,896]{1,0:T(8,128)(2,1)S(1)} %bitcast.24), channel_id=1, source_target_pairs={{0,128},{128,256},{256,384},{384,0},{1,129},{129,257},{257,385},{3... | collective-permute-start | bytes 1032200 | tf_op jit(solution)/shard_map/ppermute | solution.py:323
  57.5 5.9 %collective-permute-start.2 = (bf16[192,896]{1,0:T(8,128)(2,1)S(1)}, bf16[192,896]{1,0:T(8,128)(2,1)S(1)}, u32[]{:S(2)}, u32[]{:S(2)}) collective-permute-start(bf16[192,896]{1,0:T(8,128)(2,1)S(1)} %bitcast.20), channel_id=1, source_target_pairs={{0,384},{128,0},{256,128},{384,256},{1,385},{129,1},{257,129},{385... | collective-permute-start | bytes 1032200 | tf_op jit(solution)/shard_map/ppermute | solution.py:323
  63.3 2.2 %collective-permute-start.4 = (bf16[192,896]{1,0:T(8,128)(2,1)S(1)}, bf16[192,896]{1,0:T(8,128)(2,1)S(1)}, u32[]{:S(2)}, u32[]{:S(2)}) collective-permute-start(bf16[192,896]{1,0:T(8,128)(2,1)S(1)} %bitcast.21), channel_id=1, source_target_pairs={{0,128},{128,256},{256,384},{384,0},{1,129},{129,257},{257,385},{3... | collective-permute-start | bytes 1032200 | tf_op jit(solution)/shard_map/ppermute | solution.py:323
  65.5 5.2 %collective-permute-start.5 = (bf16[192,896]{1,0:T(8,128)(2,1)S(1)}, bf16[192,896]{1,0:T(8,128)(2,1)}, u32[]{:S(2)}, u32[]{:S(2)}) collective-permute-start(bf16[192,896]{1,0:T(8,128)(2,1)S(1)} %bitcast.25), channel_id=1, source_target_pairs={{0,384},{128,0},{256,128},{384,256},{1,385},{129,1},{257,129},{385... | collective-permute-start | bytes 1032200 | tf_op jit(solution)/shard_map/ppermute | solution.py:323
  70.7 0.0 collective-permute-done.refs_2_
  70.8 0.0 copy-start.6
  70.8 2.2 %collective-permute-start.1 = (bf16[192,896]{1,0:T(8,128)(2,1)S(1)}, bf16[192,896]{1,0:T(8,128)(2,1)S(1)}, u32[]{:S(2)}, u32[]{:S(2)}) collective-permute-start(bf16[192,896]{1,0:T(8,128)(2,1)S(1)} %collective-permute-done.refs_2_), channel_id=1, source_target_pairs={{0,128},{128,256},{256,384},{384,0},{1,129},{129,257},{257,385},{3... | collective-permute-start | bytes 1032200 | tf_op jit(solution)/shard_map/ppermute | solution.py:323
  72.9 0.7 collective-permute-done.2.refs_5_
  73.6 4.5 %collective-permute-start.3 = (bf16[192,896]{1,0:T(8,128)(2,1)S(1)}, bf16[192,896]{1,0:T(8,128)(2,1)S(1)}, u32[]{:S(2)}, u32[]{:S(2)}) collective-permute-start(bf16[192,896]{1,0:T(8,128)(2,1)S(1)} %collective-permute-done.2.refs_5_), channel_id=1, source_target_pairs={{0,384},{128,0},{256,128},{384,256},{1,385},{129,1},{257,129},{385... | collective-permute-start | bytes 1032200 | tf_op jit(solution)/shard_map/ppermute | solution.py:323
  78.2 0.0 collective-permute-done.4.refs_3_
  78.2 0.0 copy-start.8
  78.2 4.4 %collective-permute-done.5.refs_4_ = bf16[192,896]{1,0:T(8,128)(2,1)} collective-permute-done((bf16[192,896]{1,0:T(8,128)(2,1)S(1)}, bf16[192,896]{1,0:T(8,128)(2,1)}, u32[]{:S(2)}, u32[]{:S(2)}) %collective-permute-start.5) | collective-permute-done | bytes 344096 | tf_op jit(solution)/shard_map/ppermute | solution.py:323
  82.6 0.0 copy-done.1
  82.6 0.0 copy-done.2
  82.6 0.0 copy-done.6
  82.6 0.0 copy-done.7
  82.6 0.0 copy-done.8
  82.6 4.9 %shard_map.88._ = bf16[8,192,608]{2,1,0:T(8,128)(2,1)} custom-call(s32[1]{0:T(128)} %bitcast.place_ref, bf16[896,608]{1,0:T(8,128)(2,1)} %shard_map.87.weight_ref, bf16[192,896]{1,0:T(8,128)(2,1)} %bitcast.26, bf16[192,896]{1,0:T(8,128)(2,1)} %bitcast.22, bf16[192,896]{1,0:T(8,128)(2,1)} %copy-done.6, bf16[192,896]{1,0:T(8,128)(2,1)} %copy-done.8, ...), custom_call_target="tpu_custom_call" | custom-call | tf_op jit(solution)/shard_map/pallas_call | solution.py:160
  87.5 0.0 copy-done
  87.5 0.0 collective-permute-done.1.first_ref.refs_6_
  87.5 0.0 copy-start.4
  87.5 6.9 %collective-permute-done.3.second_ref.refs_7_ = bf16[192,896]{1,0:T(8,128)(2,1)S(1)} collective-permute-done((bf16[192,896]{1,0:T(8,128)(2,1)S(1)}, bf16[192,896]{1,0:T(8,128)(2,1)S(1)}, u32[]{:S(2)}, u32[]{:S(2)}) %collective-permute-start.3) | collective-permute-done | bytes 344096 | tf_op jit(solution)/shard_map/ppermute | solution.py:323
  94.4 0.0 copy-done.4
  94.4 0.7 copy-done.5
  95.2 3.0 %shard_map.89 = bf16[8,192,608]{2,1,0:T(8,128)(2,1)} custom-call(s32[1]{0:T(128)} %bitcast.place_ref, bf16[896,608]{1,0:T(8,128)(2,1)} %shard_map.87.weight_ref, bf16[192,896]{1,0:T(8,128)(2,1)} %copy-done.4, bf16[192,896]{1,0:T(8,128)(2,1)} %copy-done.5, bf16[8,192,608]{2,1,0:T(8,128)(2,1)} %shard_map.88._), custom_call_target="tpu_custom_call", output_to_operand_aliasing={{}: (4, {})} | custom-call | tf_op jit(solution)/shard_map/pallas_call | solution.py:203
  98.2 0.0 slice-start
  98.2 0.0 all-gather.3.cloned.1.call-done
  98.2 0.0 reduce-scatter.2.cloned.1.call-update
  98.2 0.9 slice-done
  99.1 29.0 %all_gather.11.rows_ref.refs_8_ = bf16[512,896]{1,0:T(8,128)(2,1)} all-gather(bf16[128,896]{1,0:T(8,128)(2,1)S(1)} %bitcast.19), channel_id=1, replica_groups=mesh['dp'=4,'edata'=8,'expert'=16] {'dp'}, dimensions={0}, use_global_device_ids=true | all-gather | bytes 1146880 | tf_op jit(solution)/shard_map/all_gather | solution.py:357
  128.1 3.4 %shard_map.90 = bf16[8,64,608]{2,1,0:T(8,128)(2,1)} custom-call(bf16[896,608]{1,0:T(8,128)(2,1)} %shard_map.87.weight_ref, bf16[512,896]{1,0:T(8,128)(2,1)} %all_gather.11.rows_ref.refs_8_), custom_call_target="tpu_custom_call" | custom-call | tf_op jit(solution)/shard_map/pallas_call | solution.py:228
  131.5 8.6 %all-to-all-start.1 = ((bf16[8,64,608]{2,1,0:T(8,128)(2,1)}), bf16[8,64,608]{2,1,0:T(8,128)(2,1)S(1)}, u32[]{:S(2)}, u32[]{:S(2)}) async-start(bf16[8,64,608]{2,1,0:T(8,128)(2,1)} %shard_map.90), calls=%async_computation.2 | async-start | bytes 1310720 | tf_op jit(solution)/shard_map/all_to_all | solution.py:358
  140.1 6.8 %shard_map.92 = bf16[608,896]{1,0:T(8,128)(2,1)} custom-call(s32[1]{0:T(128)} %bitcast.place_ref, bf16[8,608,256]{2,1,0:T(8,128)(2,1)} %bitcast.28, bf16[192,896]{1,0:T(8,128)(2,1)} %bitcast.27, bf16[192,896]{1,0:T(8,128)(2,1)} %bitcast.23, bf16[192,896]{1,0:T(8,128)(2,1)} %copy-done.6, bf16[192,896]{1,0:T(8,128)(2,1)} %copy-done.8, ...), custom_call_target="tpu_custom_call" | custom-call | tf_op jit(solution)/shard_map/pallas_call | solution.py:284
  146.9 15.7 %all-to-all-done.1.last_ref = bf16[8,64,608]{2,1,0:T(8,128)(2,1)S(1)} async-done(((bf16[8,64,608]{2,1,0:T(8,128)(2,1)}), bf16[8,64,608]{2,1,0:T(8,128)(2,1)S(1)}, u32[]{:S(2)}, u32[]{:S(2)}) %all-to-all-start.1) | async-done | bytes 622624 | tf_op jit(solution)/shard_map/all_to_all | solution.py:358
  162.6 0.9 copy-done.3
  163.4 2.3 %shard_map.91 = bf16[608,256]{1,0:T(8,128)(2,1)} custom-call(bf16[192,608]{1,0:T(8,128)(2,1)} %bitcast.33, bf16[8,64,608]{2,1,0:T(8,128)(2,1)} %copy-done.3), custom_call_target="tpu_custom_call" | custom-call | tf_op jit(solution)/shard_map/pallas_call | solution.py:312
  (4 shorter events, 0.0 us)
Async XLA Ops:
  10.7 40.5 %all-to-all-start = ((bf16[128,4,896]{2,1,0:T(4,128)(2,1)}), bf16[128,4,896]{2,1,0:T(4,128)(2,1)S(1)}, u32[]{:S(2)}, u32[]{:S(2)}) async-start(bf16[128,4,896]{2,1,0:T(4,128)(2,1)} %shard_map.86), calls=%async_computation | async-start | bytes 1835008 | tf_op jit(solution)/shard_map/all_to_all | solution.py:332
  24.9 73.2 %all-gather.3.cloned.1.call-start = ((), (), s32[]{:S(2)}) async-start(), calls=%async_computation.4 | async-start | bytes 2801664 | tf_op jit(solution)/shard_map/all_gather | solution.py:342
  51.3 111.3 %reduce-scatter.2.cloned.1.call-start = ((), (), s32[]{:S(2)}) async-start(), calls=%async_computation.3 | async-start | bytes 2211840 | tf_op jit(solution)/shard_map/reduce_scatter | solution.py:356
  51.5 35.9 %copy-start = (bf16[2,4,64,896]{3,2,1,0:T(8,128)(2,1)}, bf16[2,4,64,896]{3,2,1,0:T(8,128)(2,1)S(1)}, u32[]{:S(2)}) copy-start(bf16[2,4,64,896]{3,2,1,0:T(8,128)(2,1)S(1)} %reshape.7) | copy-start | bytes 2752516
  51.6 31.0 %copy-start.1 = (bf16[1,3,64,896]{3,2,1,0:T(8,128)(2,1)}, bf16[1,3,64,896]{3,2,1,0:T(8,128)(2,1)S(1)}, u32[]{:S(2)}) copy-start(bf16[1,3,64,896]{3,2,1,0:T(8,128)(2,1)S(1)} %get-tuple-element.14) | copy-start | bytes 1032196
  51.6 31.0 %copy-start.2 = (bf16[1,3,64,896]{3,2,1,0:T(8,128)(2,1)}, bf16[1,3,64,896]{3,2,1,0:T(8,128)(2,1)S(1)}, u32[]{:S(2)}) copy-start(bf16[1,3,64,896]{3,2,1,0:T(8,128)(2,1)S(1)} %get-tuple-element.15) | copy-start | bytes 1032196
  51.6 19.1 %collective-permute-start = (bf16[192,896]{1,0:T(8,128)(2,1)S(1)}, bf16[192,896]{1,0:T(8,128)(2,1)S(1)}, u32[]{:S(2)}, u32[]{:S(2)}) collective-permute-start(bf16[192,896]{1,0:T(8,128)(2,1)S(1)} %bitcast.24), channel_id=1, source_target_pairs={{0,128},{128,256},{256,384},{384,0},{1,129},{129,257},{257,385},{3... | collective-permute-start | bytes 1032200 | tf_op jit(solution)/shard_map/ppermute | solution.py:323
  57.5 16.2 %collective-permute-start.2 = (bf16[192,896]{1,0:T(8,128)(2,1)S(1)}, bf16[192,896]{1,0:T(8,128)(2,1)S(1)}, u32[]{:S(2)}, u32[]{:S(2)}) collective-permute-start(bf16[192,896]{1,0:T(8,128)(2,1)S(1)} %bitcast.20), channel_id=1, source_target_pairs={{0,384},{128,0},{256,128},{384,256},{1,385},{129,1},{257,129},{385... | collective-permute-start | bytes 1032200 | tf_op jit(solution)/shard_map/ppermute | solution.py:323
  63.3 14.9 %collective-permute-start.4 = (bf16[192,896]{1,0:T(8,128)(2,1)S(1)}, bf16[192,896]{1,0:T(8,128)(2,1)S(1)}, u32[]{:S(2)}, u32[]{:S(2)}) collective-permute-start(bf16[192,896]{1,0:T(8,128)(2,1)S(1)} %bitcast.21), channel_id=1, source_target_pairs={{0,128},{128,256},{256,384},{384,0},{1,129},{129,257},{257,385},{3... | collective-permute-start | bytes 1032200 | tf_op jit(solution)/shard_map/ppermute | solution.py:323
  65.5 17.1 %collective-permute-start.5 = (bf16[192,896]{1,0:T(8,128)(2,1)S(1)}, bf16[192,896]{1,0:T(8,128)(2,1)}, u32[]{:S(2)}, u32[]{:S(2)}) collective-permute-start(bf16[192,896]{1,0:T(8,128)(2,1)S(1)} %bitcast.25), channel_id=1, source_target_pairs={{0,384},{128,0},{256,128},{384,256},{1,385},{129,1},{257,129},{385... | collective-permute-start | bytes 1032200 | tf_op jit(solution)/shard_map/ppermute | solution.py:323
  70.8 11.8 %copy-start.6 = (bf16[192,896]{1,0:T(8,128)(2,1)}, bf16[192,896]{1,0:T(8,128)(2,1)S(1)}, u32[]{:S(2)}) copy-start(bf16[192,896]{1,0:T(8,128)(2,1)S(1)} %collective-permute-done.refs_2_) | copy-start | bytes 1032196
  70.8 16.7 %collective-permute-start.1 = (bf16[192,896]{1,0:T(8,128)(2,1)S(1)}, bf16[192,896]{1,0:T(8,128)(2,1)S(1)}, u32[]{:S(2)}, u32[]{:S(2)}) collective-permute-start(bf16[192,896]{1,0:T(8,128)(2,1)S(1)} %collective-permute-done.refs_2_), channel_id=1, source_target_pairs={{0,128},{128,256},{256,384},{384,0},{1,129},{129,257},{257,385},{3... | collective-permute-start | bytes 1032200 | tf_op jit(solution)/shard_map/ppermute | solution.py:323
  73.6 9.0 %copy-start.7 = (bf16[192,896]{1,0:T(8,128)(2,1)}, bf16[192,896]{1,0:T(8,128)(2,1)S(1)}, u32[]{:S(2)}) copy-start(bf16[192,896]{1,0:T(8,128)(2,1)S(1)} %collective-permute-done.2.refs_5_) | copy-start | bytes 1032196
  73.6 20.8 %collective-permute-start.3 = (bf16[192,896]{1,0:T(8,128)(2,1)S(1)}, bf16[192,896]{1,0:T(8,128)(2,1)S(1)}, u32[]{:S(2)}, u32[]{:S(2)}) collective-permute-start(bf16[192,896]{1,0:T(8,128)(2,1)S(1)} %collective-permute-done.2.refs_5_), channel_id=1, source_target_pairs={{0,384},{128,0},{256,128},{384,256},{1,385},{129,1},{257,129},{385... | collective-permute-start | bytes 1032200 | tf_op jit(solution)/shard_map/ppermute | solution.py:323
  78.2 4.4 %copy-start.8 = (bf16[192,896]{1,0:T(8,128)(2,1)}, bf16[192,896]{1,0:T(8,128)(2,1)S(1)}, u32[]{:S(2)}) copy-start(bf16[192,896]{1,0:T(8,128)(2,1)S(1)} %collective-permute-done.4.refs_3_) | copy-start | bytes 1032196
  87.5 6.9 %copy-start.4 = (bf16[192,896]{1,0:T(8,128)(2,1)}, bf16[192,896]{1,0:T(8,128)(2,1)S(1)}, u32[]{:S(2)}) copy-start(bf16[192,896]{1,0:T(8,128)(2,1)S(1)} %collective-permute-done.1.first_ref.refs_6_) | copy-start | bytes 1032196
  94.4 0.7 copy-start.5
  98.2 0.9 slice-start
  131.5 31.1 %all-to-all-start.1 = ((bf16[8,64,608]{2,1,0:T(8,128)(2,1)}), bf16[8,64,608]{2,1,0:T(8,128)(2,1)S(1)}, u32[]{:S(2)}, u32[]{:S(2)}) async-start(bf16[8,64,608]{2,1,0:T(8,128)(2,1)} %shard_map.90), calls=%async_computation.2 | async-start | bytes 1310720 | tf_op jit(solution)/shard_map/all_to_all | solution.py:358
  162.6 0.9 copy-start.3
Sparse Core Ops, SparseCore 0:
  51.4 40.1 all-gather.2
  98.3 54.0 reduce-scatter.1

commit v4 on v3

--- a/solution.py
+++ b/solution.py
@@ -10,6 +10,7 @@
 PARTS = 8
 QUARTERS = 4
 VMEM_LIMIT = 60 * 1024 * 1024
+VMEM_LITTLE = 20 * 1024 * 1024
 
 
 def full(count):
@@ -24,12 +25,12 @@
     return [pl.BlockSpec(memory_space=pltpu.SMEM)]
 
 
-def params():
-    return pltpu.CompilerParams(vmem_limit_bytes=VMEM_LIMIT)
+def params(limit=VMEM_LIMIT):
+    return pltpu.CompilerParams(vmem_limit_bytes=limit)
 
 
 def dispatch_kernel(prob_ref, ids_ref, slots_ref, counts_ref, grad_ref, out_ref, *scratch):
-    prob_v, ids_v, slots_v, counts_v, grad_v, sems = scratch
+    prob_v, ids_v, slots_v, counts_v, grad_v, out_v, sems, out_sems = scratch
     width = out_ref.shape[2]
     flight = counts_v.shape[1]
     rows = flight * CAP
@@ -70,12 +71,18 @@
             jnp.where(match, prob_v[choice : choice + 1, :], 0.0), axis=1, keepdims=True
         )
     picker = picker.astype(jnp.bfloat16)
+    stores = []
     for block in range(blocks):
         copies[4 + block].wait()
         picked = jnp.dot(picker, grad_v[block], preferred_element_type=jnp.float32)
-        out_ref[block * flight : (block + 1) * flight] = (
-            (picked * scale).reshape(flight, CAP, width).astype(out_ref.dtype)
-        )
+        window = pl.ds(block * flight, flight)
+        out_v[window] = (picked * scale).reshape(flight, CAP, width).astype(out_v.dtype)
+        stores.append(
+            pltpu.make_async_copy(out_v.at[window], out_ref.at[window], out_sems.at[block])
+        )
+        stores[-1].start()
+    for store in stores:
+        store.wait()
 
 
 def dispatch(route_prob, expert_ids, slots, counts, out_grad, blocks):
@@ -85,7 +92,7 @@
     return pl.pallas_call(
         dispatch_kernel,
         in_specs=lying(5),
-        out_specs=full(1)[0],
+        out_specs=lying(1)[0],
         out_shape=jax.ShapeDtypeStruct((blocks * flight, CAP, width), jnp.bfloat16),
         scratch_shapes=[
             pltpu.VMEM((2, tokens), jnp.float32),
@@ -93,7 +100,9 @@
             pltpu.VMEM((2, tokens), jnp.int32),
             pltpu.VMEM((1, flight), jnp.int32),
             pltpu.VMEM((blocks, tokens, width), jnp.bfloat16),
+            pltpu.VMEM((blocks * flight, CAP, width), jnp.bfloat16),
             pltpu.SemaphoreType.DMA((4 + blocks,)),
+            pltpu.SemaphoreType.DMA((blocks,)),
         ],
         compiler_params=params(),
     )(route_prob.T, expert_ids.T, slots.T, counts, out_grad)
@@ -175,26 +184,28 @@
 
 def far_kernel(place_ref, weight_ref, first_ref, second_ref, _, out_ref, *scratch):
     weight_v, far_v, far_out, sems = scratch
-    half, units = far_out.shape[1:]
+    target = place_of(place_ref[0], 2)
+    load = pltpu.make_async_copy(weight_ref, weight_v, sems.at[0])
+    load.start()
     copies = [
-        pltpu.make_async_copy(weight_ref, weight_v, sems.at[0]),
-        pltpu.make_async_copy(first_ref, far_v.at[pl.ds(0, half)], sems.at[1]),
-        pltpu.make_async_copy(second_ref, far_v.at[pl.ds(half, half)], sems.at[2]),
+        pltpu.make_async_copy(piece, far_v.at[half], sems.at[1 + half])
+        for half, piece in enumerate((first_ref, second_ref))
     ]
     for copy in copies:
         copy.start()
-    for copy in copies:
-        copy.wait()
-    far_out[...] = (
-        jnp.dot(far_v[...], weight_v[...], preferred_element_type=jnp.float32)
-        .astype(far_out.dtype)
-        .reshape(2, half, units)
-    )
-    store = pltpu.make_async_copy(
-        far_out, out_ref.at[pl.ds(place_of(place_ref[0], 2), 2)], sems.at[3]
-    )
-    store.start()
-    store.wait()
+    load.wait()
+    stores = []
+    for half in range(2):
+        copies[half].wait()
+        far_out[half] = jnp.dot(
+            far_v[half], weight_v[...], preferred_element_type=jnp.float32
+        ).astype(far_out.dtype)
+        stores.append(
+            pltpu.make_async_copy(far_out.at[half], out_ref.at[target + half], sems.at[3 + half])
+        )
+        stores[-1].start()
+    for store in stores:
+        store.wait()
 
 
 def far_partial(place, weight, far, partial):
@@ -207,9 +218,9 @@
         out_shape=jax.ShapeDtypeStruct(partial.shape, partial.dtype),
         scratch_shapes=[
             pltpu.VMEM((width, units), jnp.bfloat16),
-            pltpu.VMEM((2 * half, width), jnp.bfloat16),
+            pltpu.VMEM((2, half, width), jnp.bfloat16),
             pltpu.VMEM((2, half, units), jnp.bfloat16),
-            pltpu.SemaphoreType.DMA((4,)),
+            pltpu.SemaphoreType.DMA((5,)),
         ],
         input_output_aliases={4: 0},
         compiler_params=params(),
@@ -232,7 +243,7 @@
         out_shape=jax.ShapeDtypeStruct(
             (PARTS, rows.shape[0] // PARTS, weight.shape[1]), jnp.bfloat16
         ),
-        compiler_params=params(),
+        compiler_params=params(VMEM_LITTLE),
     )(weight, rows)
 
 
@@ -295,9 +306,12 @@
     )(place, hidden, *near, *far, *pieces)
 
 
-def finish_kernel(sums_ref, last_ref, out_ref):
+def finish_kernel(sums_ref, last_ref, out_ref, sums_v, sem):
+    copy = pltpu.make_async_copy(sums_ref, sums_v, sem)
+    copy.start()
     last = jnp.sum(last_ref[...].astype(jnp.float32), axis=0).astype(jnp.bfloat16)
-    joined = jnp.concatenate([sums_ref[...], last], axis=0)
+    copy.wait()
+    joined = jnp.concatenate([sums_v[...], last], axis=0)
     size = joined.shape[0]
     first = lax.broadcasted_iota(jnp.int32, (size, size), 0)
     second = lax.broadcasted_iota(jnp.int32, (size, size), 1)
@@ -311,10 +325,11 @@
     slots, units = sums.shape
     return pl.pallas_call(
         finish_kernel,
-        in_specs=full(2),
+        in_specs=lying(1) + full(1),
         out_specs=full(1)[0],
         out_shape=jax.ShapeDtypeStruct((units, slots + last.shape[1]), jnp.bfloat16),
-        compiler_params=params(),
+        scratch_shapes=[pltpu.VMEM(sums.shape, sums.dtype), pltpu.SemaphoreType.DMA],
+        compiler_params=params(VMEM_LITTLE),
     )(sums, last)
 
 

time: 173 us -> 172 us (level)
  waiting for transfers between devices: 51.3 us -> 53.9 us
  Pallas kernels: 26.4 us -> 23.8 us
  starting transfers between devices: 48.7 us -> 46.7 us
    all_to_all x1, waiting for transfers between devices: 15.7 us -> 18.2 us  [per_device(): lax.all_to_all(last_partial(weight, fourth), 'edata', split_axis=0, conca...]
    all_to_all x1, starting transfers between devices: 8.64 us -> 6.61 us  [per_device(): lax.all_to_all(last_partial(weight, fourth), 'edata', split_axis=0, conca...]
  transfers between devices with their start and end apart: 10 -> 10, of which waited for: 5 -> 5; matrix products, arithmetic and copies ran while one was open for 0% -> 0% of each run, Pallas kernels for 12% -> 11%
where the time goes in v4:
time: 172 us; the launch traced here: 171 us
  waiting for transfers between devices  53.9 us (31%)
  starting transfers between devices  46.7 us (27%)
  blocking collectives  29.3 us (17%)
  Pallas kernels  23.8 us (14%)
  between operations  14.3 us (8%)
  local copies, waits for them, and re-layouts  2.9 us (2%)
    all_gather x1, blocking collectives, per_device(): fourth = lax.all_gather(fourth, 'dp', axis=0, tiled=True)  29.3 us
    ppermute x6, starting transfers between devices, shifted(): lax.ppermute(value, axis, [(i, (i + step) % size) for i in range(size)])  25.8 us
    all_to_all x1, waiting for transfers between devices, per_device(): lax.all_to_all(outgoing, ('edata', 'expert'), split_axis=0, concat_axis=0...  23.6 us
    all_to_all x1, waiting for transfers between devices, per_device(): lax.all_to_all(last_partial(weight, fourth), 'edata', split_axis=0, conca...  18.2 us
    all_to_all x1, starting transfers between devices, per_device(): lax.all_to_all(outgoing, ('edata', 'expert'), split_axis=0, concat_axis=0...  14.2 us
    ppermute x6, waiting for transfers between devices, shifted(): lax.ppermute(value, axis, [(i, (i + step) % size) for i in range(size)])  12 us
    pallas_call x1, Pallas kernels, weight_grad(): pl.pallas_call(weight_kernel, in_specs=scalar() + lying(9 + len(pieces)),...  6.72 us
    all_to_all x1, starting transfers between devices, per_device(): lax.all_to_all(last_partial(weight, fourth), 'edata', split_axis=0, conca...  6.61 us
  transfers between devices with their start and end apart: 10, of which 5 were waited for; matrix products, arithmetic and copies ran while one was open for 0% of the time, Pallas kernels for 11%

profile of v4, /device:TPU:1, one launch (start us, length us, event | category | flops | bytes accessed | tf_op | source)
XLA Modules:
  0.0 170.9 jit_solution(7240212043047756305)
XLA Ops:
  7.2 3.3 %shard_map.86 = bf16[128,4,896]{2,1,0:T(4,128)(2,1)} custom-call(f32[2,128]{1,0:T(2,128)} %bitcast.34, s32[2,128]{1,0:T(2,128)} %bitcast.35, s32[2,128]{1,0:T(2,128)} %bitcast.36, s32[1,16]{1,0:T(1,128)} %counts_ref.1, bf16[128,7168]{1,0:T(8,128)(2,1)} %grad_ref.1), custom_call_target="tpu_custom_call" | custom-call | tf_op jit(solution)/shard_map/pallas_call | solution.py:92
  10.5 14.2 %all-to-all-start = ((bf16[128,4,896]{2,1,0:T(4,128)(2,1)}), bf16[128,4,896]{2,1,0:T(4,128)(2,1)S(1)}, u32[]{:S(2)}, u32[]{:S(2)}) async-start(bf16[128,4,896]{2,1,0:T(4,128)(2,1)} %shard_map.86), calls=%async_computation | async-start | bytes 1835008 | tf_op jit(solution)/shard_map/all_to_all | solution.py:347
  24.7 0.0 all-gather.3.cloned.1.call-start
  24.8 2.7 %shard_map.87.weight_ref = bf16[896,608]{1,0:T(8,128)(2,1)} custom-call(bf16[608,896]{1,0:T(8,128)(2,1)} %bitcast.30), custom_call_target="tpu_custom_call" | custom-call | tf_op jit(solution)/shard_map/pallas_call | solution.py:117
  27.4 23.6 %all-to-all-done = bf16[128,4,896]{2,1,0:T(4,128)(2,1)S(1)} async-done(((bf16[128,4,896]{2,1,0:T(4,128)(2,1)}), bf16[128,4,896]{2,1,0:T(4,128)(2,1)S(1)}, u32[]{:S(2)}, u32[]{:S(2)}) %all-to-all-start) | async-done | bytes 917536 | tf_op jit(solution)/shard_map/all_to_all | solution.py:347
  51.0 0.0 all-gather.3.cloned.1.call-update
  51.1 0.0 reduce-scatter.2.cloned.1.call-start
  51.1 0.2 reshape.7
  51.3 0.0 copy-start.3
  51.3 0.1 fusion
  51.4 0.0 copy-start.4
  51.4 0.0 copy-start.5
  51.4 5.8 %collective-permute-start = (bf16[192,896]{1,0:T(8,128)(2,1)S(1)}, bf16[192,896]{1,0:T(8,128)(2,1)S(1)}, u32[]{:S(2)}, u32[]{:S(2)}) collective-permute-start(bf16[192,896]{1,0:T(8,128)(2,1)S(1)} %bitcast.25), channel_id=1, source_target_pairs={{0,128},{128,256},{256,384},{384,0},{1,129},{129,257},{257,385},{3... | collective-permute-start | bytes 1032200 | tf_op jit(solution)/shard_map/ppermute | solution.py:338
  57.3 5.9 %collective-permute-start.2 = (bf16[192,896]{1,0:T(8,128)(2,1)S(1)}, bf16[192,896]{1,0:T(8,128)(2,1)S(1)}, u32[]{:S(2)}, u32[]{:S(2)}) collective-permute-start(bf16[192,896]{1,0:T(8,128)(2,1)S(1)} %bitcast.21), channel_id=1, source_target_pairs={{0,384},{128,0},{256,128},{384,256},{1,385},{129,1},{257,129},{385... | collective-permute-start | bytes 1032200 | tf_op jit(solution)/shard_map/ppermute | solution.py:338
  63.1 2.2 %collective-permute-start.4 = (bf16[192,896]{1,0:T(8,128)(2,1)S(1)}, bf16[192,896]{1,0:T(8,128)(2,1)S(1)}, u32[]{:S(2)}, u32[]{:S(2)}) collective-permute-start(bf16[192,896]{1,0:T(8,128)(2,1)S(1)} %bitcast.22), channel_id=1, source_target_pairs={{0,128},{128,256},{256,384},{384,0},{1,129},{129,257},{257,385},{3... | collective-permute-start | bytes 1032200 | tf_op jit(solution)/shard_map/ppermute | solution.py:338
  65.3 5.2 %collective-permute-start.5 = (bf16[192,896]{1,0:T(8,128)(2,1)S(1)}, bf16[192,896]{1,0:T(8,128)(2,1)}, u32[]{:S(2)}, u32[]{:S(2)}) collective-permute-start(bf16[192,896]{1,0:T(8,128)(2,1)S(1)} %bitcast.26), channel_id=1, source_target_pairs={{0,384},{128,0},{256,128},{384,256},{1,385},{129,1},{257,129},{385... | collective-permute-start | bytes 1032200 | tf_op jit(solution)/shard_map/ppermute | solution.py:338
  70.5 0.0 collective-permute-done.refs_2_
  70.5 0.0 copy-start.8
  70.6 2.2 %collective-permute-start.1 = (bf16[192,896]{1,0:T(8,128)(2,1)S(1)}, bf16[192,896]{1,0:T(8,128)(2,1)S(1)}, u32[]{:S(2)}, u32[]{:S(2)}) collective-permute-start(bf16[192,896]{1,0:T(8,128)(2,1)S(1)} %collective-permute-done.refs_2_), channel_id=1, source_target_pairs={{0,128},{128,256},{256,384},{384,0},{1,129},{129,257},{257,385},{3... | collective-permute-start | bytes 1032200 | tf_op jit(solution)/shard_map/ppermute | solution.py:338
  72.7 0.7 collective-permute-done.2.refs_5_
  73.4 4.5 %collective-permute-start.3 = (bf16[192,896]{1,0:T(8,128)(2,1)S(1)}, bf16[192,896]{1,0:T(8,128)(2,1)S(1)}, u32[]{:S(2)}, u32[]{:S(2)}) collective-permute-start(bf16[192,896]{1,0:T(8,128)(2,1)S(1)} %collective-permute-done.2.refs_5_), channel_id=1, source_target_pairs={{0,384},{128,0},{256,128},{384,256},{1,385},{129,1},{257,129},{385... | collective-permute-start | bytes 1032200 | tf_op jit(solution)/shard_map/ppermute | solution.py:338
  78.0 0.0 collective-permute-done.4.refs_3_
  78.0 0.0 copy-start.10
  78.0 4.4 %collective-permute-done.5.refs_4_ = bf16[192,896]{1,0:T(8,128)(2,1)} collective-permute-done((bf16[192,896]{1,0:T(8,128)(2,1)S(1)}, bf16[192,896]{1,0:T(8,128)(2,1)}, u32[]{:S(2)}, u32[]{:S(2)}) %collective-permute-start.5) | collective-permute-done | bytes 344096 | tf_op jit(solution)/shard_map/ppermute | solution.py:338
  82.4 0.0 copy-done.4
  82.4 0.0 copy-done.5
  82.4 0.0 copy-done.8
  82.4 0.0 copy-done.9
  82.4 0.0 copy-done.10
  82.4 4.8 %shard_map.88._ = bf16[8,192,608]{2,1,0:T(8,128)(2,1)} custom-call(s32[1]{0:T(128)} %bitcast.place_ref, bf16[896,608]{1,0:T(8,128)(2,1)} %shard_map.87.weight_ref, bf16[192,896]{1,0:T(8,128)(2,1)} %bitcast.27, bf16[192,896]{1,0:T(8,128)(2,1)} %bitcast.23, bf16[192,896]{1,0:T(8,128)(2,1)} %copy-done.8, bf16[192,896]{1,0:T(8,128)(2,1)} %copy-done.10, ...), custom_call_target="tpu_custom_call" | custom-call | tf_op jit(solution)/shard_map/pallas_call | solution.py:169
  87.3 0.0 copy-done.3
  87.3 0.0 collective-permute-done.1.first_ref.refs_6_
  87.3 0.0 copy-start.6
  87.3 6.9 %collective-permute-done.3.second_ref.refs_7_ = bf16[192,896]{1,0:T(8,128)(2,1)S(1)} collective-permute-done((bf16[192,896]{1,0:T(8,128)(2,1)S(1)}, bf16[192,896]{1,0:T(8,128)(2,1)S(1)}, u32[]{:S(2)}, u32[]{:S(2)}) %collective-permute-start.3) | collective-permute-done | bytes 344096 | tf_op jit(solution)/shard_map/ppermute | solution.py:338
  94.2 0.0 copy-done.6
  94.2 0.8 copy-done.7
  95.0 3.0 %shard_map.89 = bf16[8,192,608]{2,1,0:T(8,128)(2,1)} custom-call(s32[1]{0:T(128)} %bitcast.place_ref, bf16[896,608]{1,0:T(8,128)(2,1)} %shard_map.87.weight_ref, bf16[192,896]{1,0:T(8,128)(2,1)} %copy-done.6, bf16[192,896]{1,0:T(8,128)(2,1)} %copy-done.7, bf16[8,192,608]{2,1,0:T(8,128)(2,1)} %shard_map.88._), custom_call_target="tpu_custom_call", output_to_operand_aliasing={{}: (4, {})} | custom-call | tf_op jit(solution)/shard_map/pallas_call | solution.py:214
  98.0 0.0 slice-start
  98.1 0.0 all-gather.3.cloned.1.call-done
  98.1 0.0 reduce-scatter.2.cloned.1.call-update
  98.1 0.9 slice-done
  99.0 29.3 %all_gather.11.rows_ref.refs_8_ = bf16[512,896]{1,0:T(8,128)(2,1)S(1)} all-gather(bf16[128,896]{1,0:T(8,128)(2,1)S(1)} %bitcast.20), channel_id=1, replica_groups=mesh['dp'=4,'edata'=8,'expert'=16] {'dp'}, dimensions={0}, use_global_device_ids=true | all-gather | bytes 1146880 | tf_op jit(solution)/shard_map/all_gather | solution.py:372
  128.2 1.8 %shard_map.90 = bf16[8,64,608]{2,1,0:T(8,128)(2,1)} custom-call(bf16[896,608]{1,0:T(8,128)(2,1)S(1)} %copy-done, bf16[512,896]{1,0:T(8,128)(2,1)S(1)} %all_gather.11.rows_ref.refs_8_), custom_call_target="tpu_custom_call" | custom-call | tf_op jit(solution)/shard_map/pallas_call | solution.py:239
  130.0 6.6 %all-to-all-start.1 = ((bf16[8,64,608]{2,1,0:T(8,128)(2,1)}), bf16[8,64,608]{2,1,0:T(8,128)(2,1)S(1)}, u32[]{:S(2)}, u32[]{:S(2)}) async-start(bf16[8,64,608]{2,1,0:T(8,128)(2,1)} %shard_map.90), calls=%async_computation.2 | async-start | bytes 1310720 | tf_op jit(solution)/shard_map/all_to_all | solution.py:373
  136.7 6.7 %shard_map.92 = bf16[608,896]{1,0:T(8,128)(2,1)} custom-call(s32[1]{0:T(128)} %bitcast.place_ref, bf16[8,608,256]{2,1,0:T(8,128)(2,1)} %bitcast.29, bf16[192,896]{1,0:T(8,128)(2,1)} %bitcast.28, bf16[192,896]{1,0:T(8,128)(2,1)} %bitcast.24, bf16[192,896]{1,0:T(8,128)(2,1)} %copy-done.8, bf16[192,896]{1,0:T(8,128)(2,1)} %copy-done.10, ...), custom_call_target="tpu_custom_call" | custom-call | tf_op jit(solution)/shard_map/pallas_call | solution.py:295
  143.4 18.2 %all-to-all-done.1.last_ref = bf16[8,64,608]{2,1,0:T(8,128)(2,1)S(1)} async-done(((bf16[8,64,608]{2,1,0:T(8,128)(2,1)}), bf16[8,64,608]{2,1,0:T(8,128)(2,1)S(1)}, u32[]{:S(2)}, u32[]{:S(2)}) %all-to-all-start.1) | async-done | bytes 622624 | tf_op jit(solution)/shard_map/all_to_all | solution.py:373
  161.6 0.9 copy-done.2
  162.6 1.4 shard_map.91
  (8 shorter events, 0.0 us)
Async XLA Ops:
  10.5 40.5 %all-to-all-start = ((bf16[128,4,896]{2,1,0:T(4,128)(2,1)}), bf16[128,4,896]{2,1,0:T(4,128)(2,1)S(1)}, u32[]{:S(2)}, u32[]{:S(2)}) async-start(bf16[128,4,896]{2,1,0:T(4,128)(2,1)} %shard_map.86), calls=%async_computation | async-start | bytes 1835008 | tf_op jit(solution)/shard_map/all_to_all | solution.py:347
  24.7 73.3 %all-gather.3.cloned.1.call-start = ((), (), s32[]{:S(2)}) async-start(), calls=%async_computation.4 | async-start | bytes 2801664 | tf_op jit(solution)/shard_map/all_gather | solution.py:357
  51.1 110.6 %reduce-scatter.2.cloned.1.call-start = ((), (), s32[]{:S(2)}) async-start(), calls=%async_computation.3 | async-start | bytes 2211840 | tf_op jit(solution)/shard_map/reduce_scatter | solution.py:371
  51.3 35.9 %copy-start.3 = (bf16[2,4,64,896]{3,2,1,0:T(8,128)(2,1)}, bf16[2,4,64,896]{3,2,1,0:T(8,128)(2,1)S(1)}, u32[]{:S(2)}) copy-start(bf16[2,4,64,896]{3,2,1,0:T(8,128)(2,1)S(1)} %reshape.7) | copy-start | bytes 2752516
  51.4 31.0 %copy-start.4 = (bf16[1,3,64,896]{3,2,1,0:T(8,128)(2,1)}, bf16[1,3,64,896]{3,2,1,0:T(8,128)(2,1)S(1)}, u32[]{:S(2)}) copy-start(bf16[1,3,64,896]{3,2,1,0:T(8,128)(2,1)S(1)} %get-tuple-element.14) | copy-start | bytes 1032196
  51.4 31.0 %copy-start.5 = (bf16[1,3,64,896]{3,2,1,0:T(8,128)(2,1)}, bf16[1,3,64,896]{3,2,1,0:T(8,128)(2,1)S(1)}, u32[]{:S(2)}) copy-start(bf16[1,3,64,896]{3,2,1,0:T(8,128)(2,1)S(1)} %get-tuple-element.15) | copy-start | bytes 1032196
  51.4 19.1 %collective-permute-start = (bf16[192,896]{1,0:T(8,128)(2,1)S(1)}, bf16[192,896]{1,0:T(8,128)(2,1)S(1)}, u32[]{:S(2)}, u32[]{:S(2)}) collective-permute-start(bf16[192,896]{1,0:T(8,128)(2,1)S(1)} %bitcast.25), channel_id=1, source_target_pairs={{0,128},{128,256},{256,384},{384,0},{1,129},{129,257},{257,385},{3... | collective-permute-start | bytes 1032200 | tf_op jit(solution)/shard_map/ppermute | solution.py:338
  57.3 16.2 %collective-permute-start.2 = (bf16[192,896]{1,0:T(8,128)(2,1)S(1)}, bf16[192,896]{1,0:T(8,128)(2,1)S(1)}, u32[]{:S(2)}, u32[]{:S(2)}) collective-permute-start(bf16[192,896]{1,0:T(8,128)(2,1)S(1)} %bitcast.21), channel_id=1, source_target_pairs={{0,384},{128,0},{256,128},{384,256},{1,385},{129,1},{257,129},{385... | collective-permute-start | bytes 1032200 | tf_op jit(solution)/shard_map/ppermute | solution.py:338
  63.1 14.9 %collective-permute-start.4 = (bf16[192,896]{1,0:T(8,128)(2,1)S(1)}, bf16[192,896]{1,0:T(8,128)(2,1)S(1)}, u32[]{:S(2)}, u32[]{:S(2)}) collective-permute-start(bf16[192,896]{1,0:T(8,128)(2,1)S(1)} %bitcast.22), channel_id=1, source_target_pairs={{0,128},{128,256},{256,384},{384,0},{1,129},{129,257},{257,385},{3... | collective-permute-start | bytes 1032200 | tf_op jit(solution)/shard_map/ppermute | solution.py:338
  65.3 17.1 %collective-permute-start.5 = (bf16[192,896]{1,0:T(8,128)(2,1)S(1)}, bf16[192,896]{1,0:T(8,128)(2,1)}, u32[]{:S(2)}, u32[]{:S(2)}) collective-permute-start(bf16[192,896]{1,0:T(8,128)(2,1)S(1)} %bitcast.26), channel_id=1, source_target_pairs={{0,384},{128,0},{256,128},{384,256},{1,385},{129,1},{257,129},{385... | collective-permute-start | bytes 1032200 | tf_op jit(solution)/shard_map/ppermute | solution.py:338
  70.5 11.8 %copy-start.8 = (bf16[192,896]{1,0:T(8,128)(2,1)}, bf16[192,896]{1,0:T(8,128)(2,1)S(1)}, u32[]{:S(2)}) copy-start(bf16[192,896]{1,0:T(8,128)(2,1)S(1)} %collective-permute-done.refs_2_) | copy-start | bytes 1032196
  70.6 16.7 %collective-permute-start.1 = (bf16[192,896]{1,0:T(8,128)(2,1)S(1)}, bf16[192,896]{1,0:T(8,128)(2,1)S(1)}, u32[]{:S(2)}, u32[]{:S(2)}) collective-permute-start(bf16[192,896]{1,0:T(8,128)(2,1)S(1)} %collective-permute-done.refs_2_), channel_id=1, source_target_pairs={{0,128},{128,256},{256,384},{384,0},{1,129},{129,257},{257,385},{3... | collective-permute-start | bytes 1032200 | tf_op jit(solution)/shard_map/ppermute | solution.py:338
  73.4 9.0 %copy-start.9 = (bf16[192,896]{1,0:T(8,128)(2,1)}, bf16[192,896]{1,0:T(8,128)(2,1)S(1)}, u32[]{:S(2)}) copy-start(bf16[192,896]{1,0:T(8,128)(2,1)S(1)} %collective-permute-done.2.refs_5_) | copy-start | bytes 1032196
  73.4 20.8 %collective-permute-start.3 = (bf16[192,896]{1,0:T(8,128)(2,1)S(1)}, bf16[192,896]{1,0:T(8,128)(2,1)S(1)}, u32[]{:S(2)}, u32[]{:S(2)}) collective-permute-start(bf16[192,896]{1,0:T(8,128)(2,1)S(1)} %collective-permute-done.2.refs_5_), channel_id=1, source_target_pairs={{0,384},{128,0},{256,128},{384,256},{1,385},{129,1},{257,129},{385... | collective-permute-start | bytes 1032200 | tf_op jit(solution)/shard_map/ppermute | solution.py:338
  78.0 4.4 %copy-start.10 = (bf16[192,896]{1,0:T(8,128)(2,1)}, bf16[192,896]{1,0:T(8,128)(2,1)S(1)}, u32[]{:S(2)}) copy-start(bf16[192,896]{1,0:T(8,128)(2,1)S(1)} %collective-permute-done.4.refs_3_) | copy-start | bytes 1032196
  87.3 6.9 %copy-start.6 = (bf16[192,896]{1,0:T(8,128)(2,1)}, bf16[192,896]{1,0:T(8,128)(2,1)S(1)}, u32[]{:S(2)}) copy-start(bf16[192,896]{1,0:T(8,128)(2,1)S(1)} %collective-permute-done.1.first_ref.refs_6_) | copy-start | bytes 1032196
  94.2 0.8 copy-start.7
  98.0 0.9 slice-start
  98.0 30.2 %copy-start = (bf16[896,608]{1,0:T(8,128)(2,1)S(1)}, bf16[896,608]{1,0:T(8,128)(2,1)}, u32[]{:S(2)}) copy-start(bf16[896,608]{1,0:T(8,128)(2,1)} %shard_map.87.weight_ref) | copy-start | bytes 3268612
  128.2 1.8 %copy-start.1 = (bf16[512,896]{1,0:T(8,128)(2,1)}, bf16[512,896]{1,0:T(8,128)(2,1)S(1)}, u32[]{:S(2)}) copy-start(bf16[512,896]{1,0:T(8,128)(2,1)S(1)} %all_gather.11.rows_ref.refs_8_) | copy-start | bytes 2752516
  130.0 31.6 %all-to-all-start.1 = ((bf16[8,64,608]{2,1,0:T(8,128)(2,1)}), bf16[8,64,608]{2,1,0:T(8,128)(2,1)S(1)}, u32[]{:S(2)}, u32[]{:S(2)}) async-start(bf16[8,64,608]{2,1,0:T(8,128)(2,1)} %shard_map.90), calls=%async_computation.2 | async-start | bytes 1310720 | tf_op jit(solution)/shard_map/all_to_all | solution.py:373
  161.6 0.9 copy-start.2
Sparse Core Ops, SparseCore 0:
  51.2 40.1 all-gather.2
  98.2 57.7 reduce-scatter.1

commit v5 on v4

--- a/solution.py
+++ b/solution.py
@@ -185,21 +185,36 @@
 def far_kernel(place_ref, weight_ref, first_ref, second_ref, _, out_ref, *scratch):
     weight_v, far_v, far_out, sems = scratch
     target = place_of(place_ref[0], 2)
-    load = pltpu.make_async_copy(weight_ref, weight_v, sems.at[0])
-    load.start()
+    width = weight_v.shape[0]
+    cut = width // 2 // 128 * 128
+    spans = ((0, cut), (cut, width - cut))
+    loads = [
+        pltpu.make_async_copy(
+            weight_ref.at[pl.ds(*span)], weight_v.at[pl.ds(*span)], sems.at[5 * index]
+        )
+        for index, span in enumerate(spans)
+    ]
+    loads[0].start()
     copies = [
         pltpu.make_async_copy(piece, far_v.at[half], sems.at[1 + half])
         for half, piece in enumerate((first_ref, second_ref))
     ]
     for copy in copies:
         copy.start()
-    load.wait()
+    loads[1].start()
+    loads[0].wait()
     stores = []
     for half in range(2):
         copies[half].wait()
-        far_out[half] = jnp.dot(
-            far_v[half], weight_v[...], preferred_element_type=jnp.float32
-        ).astype(far_out.dtype)
+        product = jnp.dot(
+            far_v[half, :, :cut], weight_v[:cut], preferred_element_type=jnp.float32
+        )
+        if half == 0:
+            loads[1].wait()
+        product += jnp.dot(
+            far_v[half, :, cut:], weight_v[cut:], preferred_element_type=jnp.float32
+        )
+        far_out[half] = product.astype(far_out.dtype)
         stores.append(
             pltpu.make_async_copy(far_out.at[half], out_ref.at[target + half], sems.at[3 + half])
         )
@@ -220,7 +235,7 @@
             pltpu.VMEM((width, units), jnp.bfloat16),
             pltpu.VMEM((2, half, width), jnp.bfloat16),
             pltpu.VMEM((2, half, units), jnp.bfloat16),
-            pltpu.SemaphoreType.DMA((5,)),
+            pltpu.SemaphoreType.DMA((6,)),
         ],
         input_output_aliases={4: 0},
         compiler_params=params(),

time: 172 us -> 172 us (level)
  no operation moved by 1% of the time
where the time goes in v5:
time: 172 us; the launch traced here: 171 us
  waiting for transfers between devices  54 us (31%)
  starting transfers between devices  46.7 us (27%)
  blocking collectives  29.3 us (17%)
  Pallas kernels  23.9 us (14%)
  between operations  14.3 us (8%)
  local copies, waits for them, and re-layouts  2.9 us (2%)
    all_gather x1, blocking collectives, per_device(): fourth = lax.all_gather(fourth, 'dp', axis=0, tiled=True)  29.3 us
    ppermute x6, starting transfers between devices, shifted(): lax.ppermute(value, axis, [(i, (i + step) % size) for i in range(size)])  25.8 us
    all_to_all x1, waiting for transfers between devices, per_device(): lax.all_to_all(outgoing, ('edata', 'expert'), split_axis=0, concat_axis=0...  23.6 us
    all_to_all x1, waiting for transfers between devices, per_device(): lax.all_to_all(last_partial(weight, fourth), 'edata', split_axis=0, conca...  18.3 us
    all_to_all x1, starting transfers between devices, per_device(): lax.all_to_all(outgoing, ('edata', 'expert'), split_axis=0, concat_axis=0...  14.2 us
    ppermute x6, waiting for transfers between devices, shifted(): lax.ppermute(value, axis, [(i, (i + step) % size) for i in range(size)])  12 us
    pallas_call x1, Pallas kernels, weight_grad(): pl.pallas_call(weight_kernel, in_specs=scalar() + lying(9 + len(pieces)),...  6.72 us
    all_to_all x1, starting transfers between devices, per_device(): lax.all_to_all(last_partial(weight, fourth), 'edata', split_axis=0, conca...  6.6 us
  transfers between devices with their start and end apart: 10, of which 5 were waited for; matrix products, arithmetic and copies ran while one was open for 0% of the time, Pallas kernels for 11%

profile of v5, /device:TPU:1, one launch (start us, length us, event | category | flops | bytes accessed | tf_op | source)
XLA Modules:
  0.0 171.1 jit_solution(4478675344855009246)
XLA Ops:
  7.2 3.3 %shard_map.86 = bf16[128,4,896]{2,1,0:T(4,128)(2,1)} custom-call(f32[2,128]{1,0:T(2,128)} %bitcast.34, s32[2,128]{1,0:T(2,128)} %bitcast.35, s32[2,128]{1,0:T(2,128)} %bitcast.36, s32[1,16]{1,0:T(1,128)} %counts_ref.1, bf16[128,7168]{1,0:T(8,128)(2,1)} %grad_ref.1), custom_call_target="tpu_custom_call" | custom-call | tf_op jit(solution)/shard_map/pallas_call | solution.py:92
  10.5 14.2 %all-to-all-start = ((bf16[128,4,896]{2,1,0:T(4,128)(2,1)}), bf16[128,4,896]{2,1,0:T(4,128)(2,1)S(1)}, u32[]{:S(2)}, u32[]{:S(2)}) async-start(bf16[128,4,896]{2,1,0:T(4,128)(2,1)} %shard_map.86), calls=%async_computation | async-start | bytes 1835008 | tf_op jit(solution)/shard_map/all_to_all | solution.py:362
  24.7 0.0 all-gather.3.cloned.1.call-start
  24.8 2.7 %shard_map.87.weight_ref = bf16[896,608]{1,0:T(8,128)(2,1)} custom-call(bf16[608,896]{1,0:T(8,128)(2,1)} %bitcast.30), custom_call_target="tpu_custom_call" | custom-call | tf_op jit(solution)/shard_map/pallas_call | solution.py:117
  27.4 23.6 %all-to-all-done = bf16[128,4,896]{2,1,0:T(4,128)(2,1)S(1)} async-done(((bf16[128,4,896]{2,1,0:T(4,128)(2,1)}), bf16[128,4,896]{2,1,0:T(4,128)(2,1)S(1)}, u32[]{:S(2)}, u32[]{:S(2)}) %all-to-all-start) | async-done | bytes 917536 | tf_op jit(solution)/shard_map/all_to_all | solution.py:362
  51.0 0.0 all-gather.3.cloned.1.call-update
  51.1 0.0 reduce-scatter.2.cloned.1.call-start
  51.1 0.2 reshape.7
  51.3 0.0 copy-start.3
  51.3 0.1 fusion
  51.4 0.0 copy-start.4
  51.4 0.0 copy-start.5
  51.4 5.8 %collective-permute-start = (bf16[192,896]{1,0:T(8,128)(2,1)S(1)}, bf16[192,896]{1,0:T(8,128)(2,1)S(1)}, u32[]{:S(2)}, u32[]{:S(2)}) collective-permute-start(bf16[192,896]{1,0:T(8,128)(2,1)S(1)} %bitcast.25), channel_id=1, source_target_pairs={{0,128},{128,256},{256,384},{384,0},{1,129},{129,257},{257,385},{3... | collective-permute-start | bytes 1032200 | tf_op jit(solution)/shard_map/ppermute | solution.py:353
  57.3 5.9 %collective-permute-start.2 = (bf16[192,896]{1,0:T(8,128)(2,1)S(1)}, bf16[192,896]{1,0:T(8,128)(2,1)S(1)}, u32[]{:S(2)}, u32[]{:S(2)}) collective-permute-start(bf16[192,896]{1,0:T(8,128)(2,1)S(1)} %bitcast.21), channel_id=1, source_target_pairs={{0,384},{128,0},{256,128},{384,256},{1,385},{129,1},{257,129},{385... | collective-permute-start | bytes 1032200 | tf_op jit(solution)/shard_map/ppermute | solution.py:353
  63.1 2.2 %collective-permute-start.4 = (bf16[192,896]{1,0:T(8,128)(2,1)S(1)}, bf16[192,896]{1,0:T(8,128)(2,1)S(1)}, u32[]{:S(2)}, u32[]{:S(2)}) collective-permute-start(bf16[192,896]{1,0:T(8,128)(2,1)S(1)} %bitcast.22), channel_id=1, source_target_pairs={{0,128},{128,256},{256,384},{384,0},{1,129},{129,257},{257,385},{3... | collective-permute-start | bytes 1032200 | tf_op jit(solution)/shard_map/ppermute | solution.py:353
  65.3 5.2 %collective-permute-start.5 = (bf16[192,896]{1,0:T(8,128)(2,1)S(1)}, bf16[192,896]{1,0:T(8,128)(2,1)}, u32[]{:S(2)}, u32[]{:S(2)}) collective-permute-start(bf16[192,896]{1,0:T(8,128)(2,1)S(1)} %bitcast.26), channel_id=1, source_target_pairs={{0,384},{128,0},{256,128},{384,256},{1,385},{129,1},{257,129},{385... | collective-permute-start | bytes 1032200 | tf_op jit(solution)/shard_map/ppermute | solution.py:353
  70.5 0.0 collective-permute-done.refs_2_
  70.5 0.0 copy-start.8
  70.6 2.2 %collective-permute-start.1 = (bf16[192,896]{1,0:T(8,128)(2,1)S(1)}, bf16[192,896]{1,0:T(8,128)(2,1)S(1)}, u32[]{:S(2)}, u32[]{:S(2)}) collective-permute-start(bf16[192,896]{1,0:T(8,128)(2,1)S(1)} %collective-permute-done.refs_2_), channel_id=1, source_target_pairs={{0,128},{128,256},{256,384},{384,0},{1,129},{129,257},{257,385},{3... | collective-permute-start | bytes 1032200 | tf_op jit(solution)/shard_map/ppermute | solution.py:353
  72.7 0.7 collective-permute-done.2.refs_5_
  73.4 4.5 %collective-permute-start.3 = (bf16[192,896]{1,0:T(8,128)(2,1)S(1)}, bf16[192,896]{1,0:T(8,128)(2,1)S(1)}, u32[]{:S(2)}, u32[]{:S(2)}) collective-permute-start(bf16[192,896]{1,0:T(8,128)(2,1)S(1)} %collective-permute-done.2.refs_5_), channel_id=1, source_target_pairs={{0,384},{128,0},{256,128},{384,256},{1,385},{129,1},{257,129},{385... | collective-permute-start | bytes 1032200 | tf_op jit(solution)/shard_map/ppermute | solution.py:353
  78.0 0.0 collective-permute-done.4.refs_3_
  78.0 0.0 copy-start.10
  78.0 4.4 %collective-permute-done.5.refs_4_ = bf16[192,896]{1,0:T(8,128)(2,1)} collective-permute-done((bf16[192,896]{1,0:T(8,128)(2,1)S(1)}, bf16[192,896]{1,0:T(8,128)(2,1)}, u32[]{:S(2)}, u32[]{:S(2)}) %collective-permute-start.5) | collective-permute-done | bytes 344096 | tf_op jit(solution)/shard_map/ppermute | solution.py:353
  82.4 0.0 copy-done.4
  82.4 0.0 copy-done.5
  82.4 0.0 copy-done.8
  82.4 0.0 copy-done.9
  82.4 0.0 copy-done.10
  82.4 4.8 %shard_map.88._ = bf16[8,192,608]{2,1,0:T(8,128)(2,1)} custom-call(s32[1]{0:T(128)} %bitcast.place_ref, bf16[896,608]{1,0:T(8,128)(2,1)} %shard_map.87.weight_ref, bf16[192,896]{1,0:T(8,128)(2,1)} %bitcast.27, bf16[192,896]{1,0:T(8,128)(2,1)} %bitcast.23, bf16[192,896]{1,0:T(8,128)(2,1)} %copy-done.8, bf16[192,896]{1,0:T(8,128)(2,1)} %copy-done.10, ...), custom_call_target="tpu_custom_call" | custom-call | tf_op jit(solution)/shard_map/pallas_call | solution.py:169
  87.3 0.0 copy-done.3
  87.3 0.0 collective-permute-done.1.first_ref.refs_6_
  87.3 0.0 copy-start.6
  87.3 6.9 %collective-permute-done.3.second_ref.refs_7_ = bf16[192,896]{1,0:T(8,128)(2,1)S(1)} collective-permute-done((bf16[192,896]{1,0:T(8,128)(2,1)S(1)}, bf16[192,896]{1,0:T(8,128)(2,1)S(1)}, u32[]{:S(2)}, u32[]{:S(2)}) %collective-permute-start.3) | collective-permute-done | bytes 344096 | tf_op jit(solution)/shard_map/ppermute | solution.py:353
  94.2 0.0 copy-done.6
  94.2 0.8 copy-done.7
  95.0 3.1 %shard_map.89 = bf16[8,192,608]{2,1,0:T(8,128)(2,1)} custom-call(s32[1]{0:T(128)} %bitcast.place_ref, bf16[896,608]{1,0:T(8,128)(2,1)} %shard_map.87.weight_ref, bf16[192,896]{1,0:T(8,128)(2,1)} %copy-done.6, bf16[192,896]{1,0:T(8,128)(2,1)} %copy-done.7, bf16[8,192,608]{2,1,0:T(8,128)(2,1)} %shard_map.88._), custom_call_target="tpu_custom_call", output_to_operand_aliasing={{}: (4, {})} | custom-call | tf_op jit(solution)/shard_map/pallas_call | solution.py:229
  98.2 0.0 slice-start
  98.2 0.0 all-gather.3.cloned.1.call-done
  98.2 0.0 reduce-scatter.2.cloned.1.call-update
  98.2 0.9 slice-done
  99.1 29.3 %all_gather.11.rows_ref.refs_8_ = bf16[512,896]{1,0:T(8,128)(2,1)S(1)} all-gather(bf16[128,896]{1,0:T(8,128)(2,1)S(1)} %bitcast.20), channel_id=1, replica_groups=mesh['dp'=4,'edata'=8,'expert'=16] {'dp'}, dimensions={0}, use_global_device_ids=true | all-gather | bytes 1146880 | tf_op jit(solution)/shard_map/all_gather | solution.py:387
  128.4 1.8 %shard_map.90 = bf16[8,64,608]{2,1,0:T(8,128)(2,1)} custom-call(bf16[896,608]{1,0:T(8,128)(2,1)S(1)} %copy-done, bf16[512,896]{1,0:T(8,128)(2,1)S(1)} %all_gather.11.rows_ref.refs_8_), custom_call_target="tpu_custom_call" | custom-call | tf_op jit(solution)/shard_map/pallas_call | solution.py:254
  130.2 6.6 %all-to-all-start.1 = ((bf16[8,64,608]{2,1,0:T(8,128)(2,1)}), bf16[8,64,608]{2,1,0:T(8,128)(2,1)S(1)}, u32[]{:S(2)}, u32[]{:S(2)}) async-start(bf16[8,64,608]{2,1,0:T(8,128)(2,1)} %shard_map.90), calls=%async_computation.2 | async-start | bytes 1310720 | tf_op jit(solution)/shard_map/all_to_all | solution.py:388
  136.8 6.7 %shard_map.92 = bf16[608,896]{1,0:T(8,128)(2,1)} custom-call(s32[1]{0:T(128)} %bitcast.place_ref, bf16[8,608,256]{2,1,0:T(8,128)(2,1)} %bitcast.29, bf16[192,896]{1,0:T(8,128)(2,1)} %bitcast.28, bf16[192,896]{1,0:T(8,128)(2,1)} %bitcast.24, bf16[192,896]{1,0:T(8,128)(2,1)} %copy-done.8, bf16[192,896]{1,0:T(8,128)(2,1)} %copy-done.10, ...), custom_call_target="tpu_custom_call" | custom-call | tf_op jit(solution)/shard_map/pallas_call | solution.py:310
  143.5 18.3 %all-to-all-done.1.last_ref = bf16[8,64,608]{2,1,0:T(8,128)(2,1)S(1)} async-done(((bf16[8,64,608]{2,1,0:T(8,128)(2,1)}), bf16[8,64,608]{2,1,0:T(8,128)(2,1)S(1)}, u32[]{:S(2)}, u32[]{:S(2)}) %all-to-all-start.1) | async-done | bytes 622624 | tf_op jit(solution)/shard_map/all_to_all | solution.py:388
  161.8 0.9 copy-done.2
  162.8 1.4 shard_map.91
  (8 shorter events, 0.0 us)
Async XLA Ops:
  10.5 40.5 %all-to-all-start = ((bf16[128,4,896]{2,1,0:T(4,128)(2,1)}), bf16[128,4,896]{2,1,0:T(4,128)(2,1)S(1)}, u32[]{:S(2)}, u32[]{:S(2)}) async-start(bf16[128,4,896]{2,1,0:T(4,128)(2,1)} %shard_map.86), calls=%async_computation | async-start | bytes 1835008 | tf_op jit(solution)/shard_map/all_to_all | solution.py:362
  24.7 73.5 %all-gather.3.cloned.1.call-start = ((), (), s32[]{:S(2)}) async-start(), calls=%async_computation.4 | async-start | bytes 2801664 | tf_op jit(solution)/shard_map/all_gather | solution.py:372
  51.1 110.7 %reduce-scatter.2.cloned.1.call-start = ((), (), s32[]{:S(2)}) async-start(), calls=%async_computation.3 | async-start | bytes 2211840 | tf_op jit(solution)/shard_map/reduce_scatter | solution.py:386
  51.3 35.9 %copy-start.3 = (bf16[2,4,64,896]{3,2,1,0:T(8,128)(2,1)}, bf16[2,4,64,896]{3,2,1,0:T(8,128)(2,1)S(1)}, u32[]{:S(2)}) copy-start(bf16[2,4,64,896]{3,2,1,0:T(8,128)(2,1)S(1)} %reshape.7) | copy-start | bytes 2752516
  51.4 31.0 %copy-start.4 = (bf16[1,3,64,896]{3,2,1,0:T(8,128)(2,1)}, bf16[1,3,64,896]{3,2,1,0:T(8,128)(2,1)S(1)}, u32[]{:S(2)}) copy-start(bf16[1,3,64,896]{3,2,1,0:T(8,128)(2,1)S(1)} %get-tuple-element.14) | copy-start | bytes 1032196
  51.4 31.0 %copy-start.5 = (bf16[1,3,64,896]{3,2,1,0:T(8,128)(2,1)}, bf16[1,3,64,896]{3,2,1,0:T(8,128)(2,1)S(1)}, u32[]{:S(2)}) copy-start(bf16[1,3,64,896]{3,2,1,0:T(8,128)(2,1)S(1)} %get-tuple-element.15) | copy-start | bytes 1032196
  51.4 19.1 %collective-permute-start = (bf16[192,896]{1,0:T(8,128)(2,1)S(1)}, bf16[192,896]{1,0:T(8,128)(2,1)S(1)}, u32[]{:S(2)}, u32[]{:S(2)}) collective-permute-start(bf16[192,896]{1,0:T(8,128)(2,1)S(1)} %bitcast.25), channel_id=1, source_target_pairs={{0,128},{128,256},{256,384},{384,0},{1,129},{129,257},{257,385},{3... | collective-permute-start | bytes 1032200 | tf_op jit(solution)/shard_map/ppermute | solution.py:353
  57.3 16.2 %collective-permute-start.2 = (bf16[192,896]{1,0:T(8,128)(2,1)S(1)}, bf16[192,896]{1,0:T(8,128)(2,1)S(1)}, u32[]{:S(2)}, u32[]{:S(2)}) collective-permute-start(bf16[192,896]{1,0:T(8,128)(2,1)S(1)} %bitcast.21), channel_id=1, source_target_pairs={{0,384},{128,0},{256,128},{384,256},{1,385},{129,1},{257,129},{385... | collective-permute-start | bytes 1032200 | tf_op jit(solution)/shard_map/ppermute | solution.py:353
  63.1 14.9 %collective-permute-start.4 = (bf16[192,896]{1,0:T(8,128)(2,1)S(1)}, bf16[192,896]{1,0:T(8,128)(2,1)S(1)}, u32[]{:S(2)}, u32[]{:S(2)}) collective-permute-start(bf16[192,896]{1,0:T(8,128)(2,1)S(1)} %bitcast.22), channel_id=1, source_target_pairs={{0,128},{128,256},{256,384},{384,0},{1,129},{129,257},{257,385},{3... | collective-permute-start | bytes 1032200 | tf_op jit(solution)/shard_map/ppermute | solution.py:353
  65.3 17.1 %collective-permute-start.5 = (bf16[192,896]{1,0:T(8,128)(2,1)S(1)}, bf16[192,896]{1,0:T(8,128)(2,1)}, u32[]{:S(2)}, u32[]{:S(2)}) collective-permute-start(bf16[192,896]{1,0:T(8,128)(2,1)S(1)} %bitcast.26), channel_id=1, source_target_pairs={{0,384},{128,0},{256,128},{384,256},{1,385},{129,1},{257,129},{385... | collective-permute-start | bytes 1032200 | tf_op jit(solution)/shard_map/ppermute | solution.py:353
  70.5 11.8 %copy-start.8 = (bf16[192,896]{1,0:T(8,128)(2,1)}, bf16[192,896]{1,0:T(8,128)(2,1)S(1)}, u32[]{:S(2)}) copy-start(bf16[192,896]{1,0:T(8,128)(2,1)S(1)} %collective-permute-done.refs_2_) | copy-start | bytes 1032196
  70.6 16.7 %collective-permute-start.1 = (bf16[192,896]{1,0:T(8,128)(2,1)S(1)}, bf16[192,896]{1,0:T(8,128)(2,1)S(1)}, u32[]{:S(2)}, u32[]{:S(2)}) collective-permute-start(bf16[192,896]{1,0:T(8,128)(2,1)S(1)} %collective-permute-done.refs_2_), channel_id=1, source_target_pairs={{0,128},{128,256},{256,384},{384,0},{1,129},{129,257},{257,385},{3... | collective-permute-start | bytes 1032200 | tf_op jit(solution)/shard_map/ppermute | solution.py:353
  73.4 9.0 %copy-start.9 = (bf16[192,896]{1,0:T(8,128)(2,1)}, bf16[192,896]{1,0:T(8,128)(2,1)S(1)}, u32[]{:S(2)}) copy-start(bf16[192,896]{1,0:T(8,128)(2,1)S(1)} %collective-permute-done.2.refs_5_) | copy-start | bytes 1032196
  73.4 20.8 %collective-permute-start.3 = (bf16[192,896]{1,0:T(8,128)(2,1)S(1)}, bf16[192,896]{1,0:T(8,128)(2,1)S(1)}, u32[]{:S(2)}, u32[]{:S(2)}) collective-permute-start(bf16[192,896]{1,0:T(8,128)(2,1)S(1)} %collective-permute-done.2.refs_5_), channel_id=1, source_target_pairs={{0,384},{128,0},{256,128},{384,256},{1,385},{129,1},{257,129},{385... | collective-permute-start | bytes 1032200 | tf_op jit(solution)/shard_map/ppermute | solution.py:353
  78.0 4.4 %copy-start.10 = (bf16[192,896]{1,0:T(8,128)(2,1)}, bf16[192,896]{1,0:T(8,128)(2,1)S(1)}, u32[]{:S(2)}) copy-start(bf16[192,896]{1,0:T(8,128)(2,1)S(1)} %collective-permute-done.4.refs_3_) | copy-start | bytes 1032196
  87.3 6.9 %copy-start.6 = (bf16[192,896]{1,0:T(8,128)(2,1)}, bf16[192,896]{1,0:T(8,128)(2,1)S(1)}, u32[]{:S(2)}) copy-start(bf16[192,896]{1,0:T(8,128)(2,1)S(1)} %collective-permute-done.1.first_ref.refs_6_) | copy-start | bytes 1032196
  94.2 0.8 copy-start.7
  98.2 0.9 slice-start
  98.2 30.2 %copy-start = (bf16[896,608]{1,0:T(8,128)(2,1)S(1)}, bf16[896,608]{1,0:T(8,128)(2,1)}, u32[]{:S(2)}) copy-start(bf16[896,608]{1,0:T(8,128)(2,1)} %shard_map.87.weight_ref) | copy-start | bytes 3268612
  128.4 1.8 %copy-start.1 = (bf16[512,896]{1,0:T(8,128)(2,1)}, bf16[512,896]{1,0:T(8,128)(2,1)S(1)}, u32[]{:S(2)}) copy-start(bf16[512,896]{1,0:T(8,128)(2,1)S(1)} %all_gather.11.rows_ref.refs_8_) | copy-start | bytes 2752516
  130.2 31.7 %all-to-all-start.1 = ((bf16[8,64,608]{2,1,0:T(8,128)(2,1)}), bf16[8,64,608]{2,1,0:T(8,128)(2,1)S(1)}, u32[]{:S(2)}, u32[]{:S(2)}) async-start(bf16[8,64,608]{2,1,0:T(8,128)(2,1)} %shard_map.90), calls=%async_computation.2 | async-start | bytes 1310720 | tf_op jit(solution)/shard_map/all_to_all | solution.py:388
  161.8 0.9 copy-start.2
Sparse Core Ops, SparseCore 0:
  51.2 40.1 all-gather.2
  98.4 57.7 reduce-scatter.1
